TPU v7x, 256 devices: a whole 4x4x8 slice. The times are simulated.
256 devices in a mesh: batch: 64 (over y_hi, x, z), rep: 4 (over y_lo, core).
Axes of the slice: x: 4, y: 4 (y_hi: 2, y_lo: 2; y = y_hi * 2 + y_lo), z: 8, core: 2. Of those that a mesh axis runs over, the one named last changes fastest.
Arguments:
- query_hidden: bfloat16 [4, 8192, 4096], P('rep', 'batch'), may hold values from -2 to 2
- passage_hidden: bfloat16 [4, 8192, 4096], P('rep', 'batch'), may hold values from -2 to 2
- norm_gain: float32 [4096], replicated, may hold values from 0.1 to 1.9
- negatives: int32 [4, 8192, 3], P('rep', 'batch'), may hold values from 0 to 8191, as said below
Outputs:
- query_grad: float32 [4, 8192, 4096], P('rep', 'batch')
- passage_grad: float32 [4, 8192, 4096], P('rep', 'batch')
- query_loss: float32 [4, 8192], P('rep', 'batch')
- gain_grad: float32 [4096], replicated
Inputs may be any that keep to these rules, and one draw needn't show every extreme that they name: `negatives`: entries name passages of the query's own group; passage j lies on device j // 128 of batch, at row j % 128. The 384 entries of one device name any one owner at most 14 times and name at most 7 different passages of it. In every draw one owner is named exactly 14 times, through exactly 7 different passages, by every device of the group.
All inputs are finite; a program needn't handle non-finite values.
Results may differ from a plain program's by a relative error of at most 0.0047.
Values may be sent and summed in bfloat16 or wider, within the bound.
A program may use at most 128 MiB of HBM per device.

v0:
```python
import jax
import jax.numpy as jnp
from jax import lax
from jax.sharding import PartitionSpec as P

STOPS = 4


TEMP = 0.05
EPS = 1e-06


def from_behind(block, axis, distance):
    devices = range(lax.axis_size(axis))
    route = [((i - distance) % len(devices), i) for i in devices]
    return lax.ppermute(block, axis, route)


def unit_rows(hidden, norm_gain):
    scaled = hidden.astype(jnp.float32) * norm_gain
    length = jnp.sqrt(jnp.sum(scaled * scaled, axis=-1, keepdims=True) + EPS)
    return (scaled / length, length)


def norm_back(grad_rows, direct, length, hidden, norm_gain):
    inner_prod = jnp.sum(direct * grad_rows, axis=-1, keepdims=True)
    dscaled = (grad_rows - direct * inner_prod) / length
    return (dscaled * norm_gain, jnp.sum(hidden.astype(jnp.float32) * dscaled, axis=0))


def pick_slots(member):
    rank_table = jnp.cumsum(member, axis=0) - 1
    return jnp.sum(rank_table * member, axis=1)


def local(query_hidden, passage_hidden, norm_gain, negatives):
    q_hidden = query_hidden[0]
    p_hidden = passage_hidden[0]
    wanted = negatives[0]
    row_count, feat_width = q_hidden.shape
    neg_count = wanted.shape[1]
    peer_count = lax.axis_size("batch")
    request_count = row_count * neg_count
    unique_cap = (request_count + peer_count - 1) // peer_count + 1
    capacity = 2 * unique_cap
    q_dir, q_len = unit_rows(q_hidden, norm_gain)
    p_dir, p_len = unit_rows(p_hidden, norm_gain)
    q_emb = q_dir.astype(jnp.bfloat16)
    p_emb = p_dir.astype(jnp.bfloat16)
    blocks = [p_emb]
    for stop_index in range(1, STOPS):
        blocks.append(from_behind(blocks[-1], "batch", 1))
    window = jnp.concatenate(blocks, axis=0)
    flat_index = wanted.reshape(request_count)
    owner_dev = flat_index // row_count
    local_row = flat_index % row_count
    peer_ids = jnp.arange(peer_count, dtype=jnp.int32)
    member = (owner_dev[:, None] == peer_ids[None, :]).astype(jnp.int32)
    slot_each = pick_slots(member)
    same_index = (flat_index[:, None] == flat_index[None, :]).astype(jnp.int32)
    first_seen = jnp.argmax(same_index, axis=1)
    leader = first_seen == jnp.arange(request_count, dtype=jnp.int32)
    request = (
        jnp.full((peer_count, capacity), row_count, jnp.int32)
        .at[owner_dev, slot_each]
        .set(local_row)
    )
    asked_rows = lax.all_to_all(request, "batch", split_axis=0, concat_axis=0, tiled=True)
    found_rows = jnp.take(p_emb, jnp.minimum(asked_rows, row_count - 1), axis=0)
    arrived = lax.all_to_all(found_rows, "batch", split_axis=0, concat_axis=0, tiled=True)
    fetched = arrived[owner_dev, slot_each]
    fetched_rows = fetched.reshape(row_count, neg_count, feat_width)
    scores = jnp.einsum("td,jd->tj", q_emb, window, preferred_element_type=jnp.float32) / TEMP
    neg_scores = (
        jnp.einsum("td,tkd->tk", q_emb, fetched_rows, preferred_element_type=jnp.float32) / TEMP
    )
    exp_scores = jnp.exp(scores)
    exp_negative = jnp.exp(neg_scores)
    partition = jnp.sum(exp_scores, axis=1) + jnp.sum(exp_negative, axis=1)
    inverse = 1.0 / partition
    query_loss = jnp.log(partition) - jnp.diagonal(scores[:, :row_count])
    identity = jnp.eye(row_count, STOPS * row_count, dtype=jnp.float32)
    weight = (exp_scores * inverse[:, None] - identity).astype(jnp.bfloat16)
    neg_weight = (exp_negative * inverse[:, None]).astype(jnp.bfloat16)
    q_grad = (
        jnp.dot(weight, window, preferred_element_type=jnp.float32)
        + jnp.einsum("tk,tkd->td", neg_weight, fetched_rows, preferred_element_type=jnp.float32)
    ) / TEMP
    block_all = jnp.einsum("tj,td->jd", weight, q_emb, preferred_element_type=jnp.float32) / TEMP
    p_grad = block_all[:row_count]
    far_terms = block_all[row_count:].astype(jnp.bfloat16).reshape(STOPS - 1, row_count, feat_width)
    for stop_index in range(1, STOPS):
        back_term = from_behind(far_terms[stop_index - 1], "batch", -stop_index)
        p_grad = p_grad + back_term.astype(jnp.float32)
    neg_rows = (
        neg_weight.astype(jnp.float32)[:, :, None] * q_emb.astype(jnp.float32)[:, None, :] / TEMP
    )
    neg_rows = neg_rows.reshape(request_count, feat_width)
    targets = jnp.arange(row_count, dtype=jnp.int32)
    summed = jnp.dot(
        same_index.astype(jnp.float32),
        neg_rows,
        precision=lax.Precision.HIGHEST,
        preferred_element_type=jnp.float32,
    )
    summed = jnp.where(leader[:, None], summed, 0.0).astype(jnp.bfloat16)
    outgoing = (
        jnp.zeros((peer_count, capacity, feat_width), jnp.bfloat16)
        .at[owner_dev, slot_each]
        .set(summed)
    )
    returned = lax.all_to_all(outgoing, "batch", split_axis=0, concat_axis=0, tiled=True)
    hit_table = (asked_rows.reshape(-1)[None, :] == targets[:, None]).astype(jnp.bfloat16)
    p_grad = p_grad + jnp.dot(
        hit_table, returned.reshape(-1, feat_width), preferred_element_type=jnp.float32
    )
    query_grad, gain_query = norm_back(q_grad, q_dir, q_len, q_hidden, norm_gain)
    passage_grad, gain_passage = norm_back(p_grad, p_dir, p_len, p_hidden, norm_gain)
    gain_grad = lax.psum(gain_query + gain_passage, ("batch", "rep"))
    return (query_grad[None], passage_grad[None], query_loss[None], gain_grad)


def solution(mesh):
    return jax.shard_map(
        local,
        mesh=mesh,
        in_specs=(P("rep", "batch", None), P("rep", "batch", None), P(), P("rep", "batch", None)),
        out_specs=(P("rep", "batch", None), P("rep", "batch", None), P("rep", "batch"), P()),
        check_vma=False,
    )
```

profile of v0, /device:TPU:1, one launch (start us, length us, event | category | flops | bytes accessed | tf_op | source)
XLA Modules:
  0.0 937.9 jit_solution(1588705214250921376)
XLA Ops:
  0.6 0.8 copy.27
  2.1 0.9 reduce-window.6
  3.5 20.4 %scatter_fusion = s32[64,14]{0,1:T(8,128)S(1)} fusion(s32[64,14]{0,1:T(8,128)S(1)} %broadcast_in_dim.36, s32[384]{0:T(512)S(1)} %get-tuple-element.11, s32[384]{0:T(512)S(1)} %get-tuple-element.25), kind=kCustom, calls=%fused_computation.3 | custom fusion | bytes 7680 | tf_op jit(solution)/shard_map/scatter | solution.py:66
  24.6 15.1 %all-to-all-start = ((s32[64,1,14]{2,1,0:T(1,128)}), s32[64,1,14]{2,1,0:T(1,128)S(1)}, u32[]{:S(2)}, u32[]{:S(2)}) async-start(s32[64,1,14]{2,1,0:T(1,128)} %copy.31), calls=%async_computation | async-start | bytes 65536 | tf_op jit(solution)/shard_map/all_to_all | solution.py:68
  40.4 2.3 fusion.44
  42.7 7.8 all-to-all-done
  50.9 6.7 gather_fusion
  57.6 9.3 reshape.271
  66.9 7.4 broadcast_select_fusion
  74.4 5.7 all-to-all-start.1
  80.1 0.9 collective-permute-start
  81.0 207.6 %collective-permute-done = bf16[128,4096]{1,0:T(8,128)(2,1)S(1)} collective-permute-done((bf16[128,4096]{1,0:T(8,128)(2,1)S(1)}, bf16[128,4096]{1,0:T(8,128)(2,1)S(1)}, u32[]{:S(2)}, u32[]{:S(2)}) %collective-permute-start) | collective-permute-done | bytes 1048608 | tf_op jit(solution)/shard_map/ppermute | solution.py:16
  288.7 1.0 copy-done.6
  289.6 28.5 %collective-permute-done.1 = bf16[128,4096]{1,0:T(8,128)(2,1)} collective-permute-done((bf16[128,4096]{1,0:T(8,128)(2,1)S(1)}, bf16[128,4096]{1,0:T(8,128)(2,1)}, u32[]{:S(2)}, u32[]{:S(2)}) %collective-permute-start.1) | collective-permute-done | bytes 1048608 | tf_op jit(solution)/shard_map/ppermute | solution.py:16
  318.1 7.2 mul.120
  325.3 9.6 %mul.121 = f32[384,4096]{1,0:T(8,128)} reshape(f32[128,3,4096]{2,1,0:T(4,128)} %mul.120) | data formatting | bytes 12582912 | tf_op jit(solution)/shard_map/mul | solution.py:96
  335.0 0.9 convert_reduce_fusion
  335.9 10.0 %collective-permute-done.2 = bf16[128,4096]{1,0:T(8,128)(2,1)} collective-permute-done((bf16[128,4096]{1,0:T(8,128)(2,1)}, bf16[128,4096]{1,0:T(8,128)(2,1)}, u32[]{:S(2)}, u32[]{:S(2)}) %collective-permute-start.2) | collective-permute-done | bytes 1048608 | tf_op jit(solution)/shard_map/ppermute | solution.py:16
  345.9 3.7 exponential_reduce_fusion
  349.6 1.2 gather_fusion.2
  350.9 10.4 %copy.35 = bf16[64,14,4096]{2,0,1:T(8,128)(2,1)} copy(bf16[64,14,4096]{2,1,0:T(8,128)(2,1)} %all-to-all-done.1) | data formatting | bytes 14680064 | tf_op jit(solution)/shard_map/all_to_all | solution.py:70
  361.3 17.7 %gather_fusion.1 = bf16[384,4096]{1,0:T(8,128)(2,1)} fusion(bf16[64,14,4096]{2,0,1:T(8,128)(2,1)} %copy.35, s32[384]{0:T(512)S(1)} %get-tuple-element.10), kind=kCustom, calls=%fused_computation.1 | custom fusion | bytes 6294528 | tf_op jit(solution)/shard_map/gather | solution.py:71
  379.0 7.2 reshape.265
  386.2 8.0 fusion.19
  394.9 0.7 fusion.40
  395.6 1.0 reshape.269
  396.7 14.1 %select_convert_fusion = bf16[384,4096]{1,0:T(8,128)(2,1)} fusion(f32[384,4096]{1,0:T(8,128)} %mul.121, f32[384]{0:T(512)S(1)} %reshape.269, pred[384]{0:T(512)(128)(4,1)S(1)} %iota_compare_fusion.7, s32[384]{0:T(512)S(1)} %reshape_squeeze.8), kind=kOutput, calls=%fused_computation.7 | convolution fusion | flops 7254491136 | bytes 9440640 | tf_op jit(solution)/shard_map/dot_general | solution.py:100
  410.7 3.9 broadcast_in_dim.41
  414.6 101.3 %scatter_fusion.1 = bf16[64,14,4096]{2,0,1:T(8,128)(2,1)} fusion(bf16[64,14,4096]{2,0,1:T(8,128)(2,1)} %broadcast_in_dim.41, s32[384]{0:T(512)S(1)} %get-tuple-element.11, bf16[384,4096]{1,0:T(8,128)(2,1)} %select_convert_fusion), kind=kCustom, calls=%fused_computation.4 | custom fusion | bytes 9440256 | tf_op jit(solution)/shard_map/scatter | solution.py:110
  515.9 10.4 %copy.36 = bf16[64,14,4096]{2,1,0:T(8,128)(2,1)} copy(bf16[64,14,4096]{2,0,1:T(8,128)(2,1)} %scatter_fusion.1) | data formatting | bytes 14680064 | tf_op jit(solution)/shard_map/scatter | solution.py:110
  526.3 5.8 all-to-all-start.2
  532.0 4.6 fusion.49
  536.7 1.8 fusion.48
  538.5 8.8 collective-permute-start.5
  547.2 1.2 collective-permute-start.4
  549.3 0.7 reduce.28
  550.2 4.6 fusion.28
  554.8 4.9 fusion.5
  559.8 151.6 %all-to-all-done.2 = bf16[64,14,4096]{2,1,0:T(8,128)(2,1)} async-done(((bf16[64,14,4096]{2,1,0:T(8,128)(2,1)}), bf16[64,14,4096]{2,1,0:T(8,128)(2,1)}, u32[]{:S(2)}, u32[]{:S(2)}) %all-to-all-start.2) | async-done | bytes 7340064 | tf_op jit(solution)/shard_map/all_to_all | solution.py:112
  711.4 9.3 reshape.266
  720.7 50.0 %collective-permute-done.5 = bf16[128,4096]{1,0:T(8,128)(2,1)} collective-permute-done((bf16[128,4096]{1,0:T(8,128)(2,1)}, bf16[128,4096]{1,0:T(8,128)(2,1)}, u32[]{:S(2)}, u32[]{:S(2)}) %collective-permute-start.5) | collective-permute-done | bytes 1048608 | tf_op jit(solution)/shard_map/ppermute | solution.py:16
  770.7 51.9 %collective-permute-done.4 = bf16[128,4096]{1,0:T(8,128)(2,1)} collective-permute-done((bf16[128,4096]{1,0:T(8,128)(2,1)}, bf16[128,4096]{1,0:T(8,128)(2,1)}, u32[]{:S(2)}, u32[]{:S(2)}) %collective-permute-start.4) | collective-permute-done | bytes 1048608 | tf_op jit(solution)/shard_map/ppermute | solution.py:16
  822.6 23.5 %collective-permute-done.3 = bf16[128,4096]{1,0:T(8,128)(2,1)} collective-permute-done((bf16[128,4096]{1,0:T(8,128)(2,1)}, bf16[128,4096]{1,0:T(8,128)(2,1)}, u32[]{:S(2)}, u32[]{:S(2)}) %collective-permute-start.3) | collective-permute-done | bytes 1048608 | tf_op jit(solution)/shard_map/ppermute | solution.py:16
  846.1 7.8 multiply_reduce_fusion
  854.6 0.9 copy-done.2
  855.5 2.1 fusion.14
  857.6 1.5 multiply_bitcast_fusion.1
  859.1 78.6 %psum.7 = f32[4096]{0:T(1024)} all-reduce(f32[4096]{0:T(1024)S(1)} %add.130), channel_id=1, replica_groups=mesh['batch'=64,'rep'=4] {'batch','rep'}, use_global_device_ids=true, to_apply=%region_14.15 | all-reduce | flops 4096 | bytes 32768 | tf_op jit(solution)/shard_map/psum | solution.py:119
  (48 shorter events, 5.3 us)
Async XLA Ops:
  3.4 36.3 %copy-start = (bf16[1,128,4096]{2,1,0:T(8,128)(2,1)S(1)}, bf16[1,128,4096]{2,1,0:T(8,128)(2,1)}, u32[]{:S(2)}) copy-start(bf16[1,128,4096]{2,1,0:T(8,128)(2,1)} %param.4) | copy-start | bytes 3145732
  3.4 36.3 %copy-start.1 = (bf16[1,128,4096]{2,1,0:T(8,128)(2,1)S(1)}, bf16[1,128,4096]{2,1,0:T(8,128)(2,1)}, u32[]{:S(2)}) copy-start(bf16[1,128,4096]{2,1,0:T(8,128)(2,1)} %param.5) | copy-start | bytes 3145732
  3.5 36.3 %copy-start.3 = (f32[4096]{0:T(1024)S(1)}, f32[4096]{0:T(1024)}, u32[]{:S(2)}) copy-start(f32[4096]{0:T(1024)} %param.6) | copy-start | bytes 49156
  24.6 25.9 %all-to-all-start = ((s32[64,1,14]{2,1,0:T(1,128)}), s32[64,1,14]{2,1,0:T(1,128)S(1)}, u32[]{:S(2)}, u32[]{:S(2)}) async-start(s32[64,1,14]{2,1,0:T(1,128)} %copy.31), calls=%async_computation | async-start | bytes 65536 | tf_op jit(solution)/shard_map/all_to_all | solution.py:68
  74.4 276.5 %all-to-all-start.1 = ((bf16[64,14,4096]{2,1,0:T(8,128)(2,1)}), bf16[64,14,4096]{2,1,0:T(8,128)(2,1)}, u32[]{:S(2)}, u32[]{:S(2)}) async-start(bf16[64,14,4096]{2,1,0:T(8,128)(2,1)} %broadcast_select_fusion), calls=%async_computation.1 | async-start | bytes 16777216 | tf_op jit(solution)/shard_map/all_to_all | solution.py:70
  80.1 208.5 %collective-permute-start = (bf16[128,4096]{1,0:T(8,128)(2,1)S(1)}, bf16[128,4096]{1,0:T(8,128)(2,1)S(1)}, u32[]{:S(2)}, u32[]{:S(2)}) collective-permute-start(bf16[128,4096]{1,0:T(8,128)(2,1)S(1)} %get-tuple-element.24), channel_id=1, source_target_pairs={{252,0},{0,4},{4,8},{8,12},{12,16},{16,20},{20,24},{24,28},{28,32}... | collective-permute-start | bytes 3145736 | tf_op jit(solution)/shard_map/ppermute | solution.py:16
  288.7 1.0 copy-start.6
  289.6 28.5 %collective-permute-start.1 = (bf16[128,4096]{1,0:T(8,128)(2,1)S(1)}, bf16[128,4096]{1,0:T(8,128)(2,1)}, u32[]{:S(2)}, u32[]{:S(2)}) collective-permute-start(bf16[128,4096]{1,0:T(8,128)(2,1)S(1)} %collective-permute-done), channel_id=1, source_target_pairs={{252,0},{0,4},{4,8},{8,12},{12,16},{16,20},{20,24},{24,28},{28,32}... | collective-permute-start | bytes 3145736 | tf_op jit(solution)/shard_map/ppermute | solution.py:16
  318.1 27.8 %collective-permute-start.2 = (bf16[128,4096]{1,0:T(8,128)(2,1)}, bf16[128,4096]{1,0:T(8,128)(2,1)}, u32[]{:S(2)}, u32[]{:S(2)}) collective-permute-start(bf16[128,4096]{1,0:T(8,128)(2,1)} %collective-permute-done.1), channel_id=1, source_target_pairs={{252,0},{0,4},{4,8},{8,12},{12,16},{16,20},{20,24},{24,28},{28,32}... | collective-permute-start | bytes 3145736 | tf_op jit(solution)/shard_map/ppermute | solution.py:16
  386.2 8.2 copy-start.5
  526.3 185.1 %all-to-all-start.2 = ((bf16[64,14,4096]{2,1,0:T(8,128)(2,1)}), bf16[64,14,4096]{2,1,0:T(8,128)(2,1)}, u32[]{:S(2)}, u32[]{:S(2)}) async-start(bf16[64,14,4096]{2,1,0:T(8,128)(2,1)} %copy.36), calls=%async_computation.2 | async-start | bytes 16777216 | tf_op jit(solution)/shard_map/all_to_all | solution.py:112
  536.7 13.6 %copy-start.4 = (bf16[128,3,1]{1,0,2:T(8,128)(2,1)S(1)}, bf16[128,3,1]{1,0,2:T(8,128)(2,1)}, u32[]{:S(2)}) copy-start(bf16[128,3,1]{1,0,2:T(8,128)(2,1)} %get-tuple-element.22) | copy-start | bytes 2308
  538.5 232.2 %collective-permute-start.5 = (bf16[128,4096]{1,0:T(8,128)(2,1)}, bf16[128,4096]{1,0:T(8,128)(2,1)}, u32[]{:S(2)}, u32[]{:S(2)}) collective-permute-start(bf16[128,4096]{1,0:T(8,128)(2,1)} %get-tuple-element.17), channel_id=1, source_target_pairs={{12,0},{16,4},{20,8},{24,12},{28,16},{32,20},{36,24},{40,28},{44,3... | collective-permute-start | bytes 3145736 | tf_op jit(solution)/shard_map/ppermute | solution.py:16
  547.2 275.4 %collective-permute-start.4 = (bf16[128,4096]{1,0:T(8,128)(2,1)}, bf16[128,4096]{1,0:T(8,128)(2,1)}, u32[]{:S(2)}, u32[]{:S(2)}) collective-permute-start(bf16[128,4096]{1,0:T(8,128)(2,1)} %get-tuple-element.18), channel_id=1, source_target_pairs={{8,0},{12,4},{16,8},{20,12},{24,16},{28,20},{32,24},{36,28},{40,32... | collective-permute-start | bytes 3145736 | tf_op jit(solution)/shard_map/ppermute | solution.py:16
  548.4 297.7 %collective-permute-start.3 = (bf16[128,4096]{1,0:T(8,128)(2,1)}, bf16[128,4096]{1,0:T(8,128)(2,1)}, u32[]{:S(2)}, u32[]{:S(2)}) collective-permute-start(bf16[128,4096]{1,0:T(8,128)(2,1)} %get-tuple-element.16), channel_id=1, source_target_pairs={{4,0},{8,4},{12,8},{16,12},{20,16},{24,20},{28,24},{32,28},{36,32}... | collective-permute-start | bytes 3145736 | tf_op jit(solution)/shard_map/ppermute | solution.py:16
  550.2 4.6 copy-start.7
  853.9 1.6 copy-start.2
where the time goes:
time: 948 us; the launch traced here: 938 us
  waiting for transfers between devices  531 us (56%)
  local copies, waits for them, and re-layouts  223 us (24%)
  blocking collectives  78.6 us (8%)
  matrix products  47.8 us (5%)
  starting transfers between devices  37.9 us (4%)
  other arithmetic  18.8 us (2%)
    ppermute x6, waiting for transfers between devices, from_behind(): return lax.ppermute(block, axis, route)  372 us
    all_to_all x1, waiting for transfers between devices, local(): lax.all_to_all(outgoing, 'batch', split_axis=0, concat_axis=0, tiled=True)  152 us
    scatter x2, local copies, waits for them, and re-layouts, local(): outgoing = jnp.zeros((peer_count, capacity, feat_width), jnp.bfloat16).at...  112 us
    psum x1, blocking collectives, local(): gain_grad = lax.psum(gain_query + gain_passage, ('batch', 'rep'))  78.6 us
    scatter x1, local copies, waits for them, and re-layouts, local(): request = jnp.full((peer_count, capacity), row_count, jnp.int32).at[owner...  20.4 us
  transfers between devices with their start and end apart: 9, of which 8 were waited for; matrix products, arithmetic and copies ran while one was open for 6% of the time, Pallas kernels for 0%

commit v1 on v0

v1 whole, which is shorter than its diff:
```python
import functools

import jax
import jax.numpy as jnp
from jax import lax
from jax.experimental import pallas as pl
from jax.experimental.pallas import tpu as pltpu
from jax.sharding import PartitionSpec as P

STOPS = 4
TEMP = 0.05
EPS = 1e-06
SLOTS = 8
MIB = 1 << 20


def from_behind(block, axis, distance):
    size = lax.axis_size(axis)
    route = [((i - distance) % size, i) for i in range(size)]
    return lax.ppermute(block, axis, route)


def norm_kernel(q_ref, p_ref, gain_ref, qe_ref, pe_ref, x_ref, qn_ref, pn_ref):
    gain = gain_ref[...]
    units = []
    for src, emb, norm in ((q_ref, qe_ref, qn_ref), (p_ref, pe_ref, pn_ref)):
        scaled = src[...].astype(jnp.float32) * gain
        length = jnp.sqrt(jnp.sum(scaled * scaled, axis=-1, keepdims=True) + EPS)
        unit = scaled * (1.0 / length)
        emb[...] = unit.astype(jnp.bfloat16)
        norm[...] = jnp.broadcast_to(length, norm.shape)
        units.append(unit)
    q_unit, p_unit = units
    low = lax.broadcasted_iota(jnp.int32, (q_ref.shape[0], 128), 1) < 64
    for tile in range(q_ref.shape[1] // 128):
        q_tile = q_unit[:, tile * 128 : (tile + 1) * 128]
        p_tile = p_unit[:, tile * 128 : (tile + 1) * 128]
        x_ref[2 * tile] = jnp.where(low, q_tile, pltpu.roll(p_tile, 64, 1)).astype(jnp.bfloat16)
        x_ref[2 * tile + 1] = jnp.where(low, pltpu.roll(q_tile, 64, 1), p_tile).astype(jnp.bfloat16)


def normalize(q_hidden, p_hidden, gain):
    rows, width = q_hidden.shape
    tiles = width // 64
    step = 32
    row_block = pl.BlockSpec((step, width), lambda i: (i, 0))
    norm_block = pl.BlockSpec((step, 128), lambda i: (i, 0))
    return pl.pallas_call(
        norm_kernel,
        grid=(rows // step,),
        in_specs=[row_block, row_block, pl.BlockSpec((1, width), lambda i: (0, 0))],
        out_specs=[
            row_block,
            row_block,
            pl.BlockSpec((tiles, step, 128), lambda i: (0, i, 0)),
            norm_block,
            norm_block,
        ],
        out_shape=[
            jax.ShapeDtypeStruct((rows, width), jnp.bfloat16),
            jax.ShapeDtypeStruct((rows, width), jnp.bfloat16),
            jax.ShapeDtypeStruct((tiles, rows, 128), jnp.bfloat16),
            jax.ShapeDtypeStruct((rows, 128), jnp.float32),
            jax.ShapeDtypeStruct((rows, 128), jnp.float32),
        ],
        compiler_params=pltpu.CompilerParams(vmem_limit_bytes=32 * MIB),
        cost_estimate=pl.CostEstimate(flops=10 * rows * width, bytes_accessed=10 * rows * width, transcendentals=0),
        name="normalize",
    )(q_hidden, p_hidden, gain.reshape(1, width))


def neg_forward_kernel(half, hot_ref, w_ref, slot_ref, t_ref, table_ref, scratch):
    step = pl.program_id(0)

    @pl.when(step < half)
    def _():
        picked = []
        for part in range(2):
            rows = jnp.dot(hot_ref[part], w_ref[2 * step + part], preferred_element_type=jnp.float32)
            picked.append(rows.reshape(-1, SLOTS, 128))
        both = jnp.concatenate(picked, axis=1).astype(jnp.bfloat16)
        scratch[:, pl.ds(pl.multiple_of(step * 16, 16), 16), :] = both

    @pl.when(step >= half)
    def _():
        pair = step - half
        for part in range(2):
            device = 2 * pair + part
            table = scratch[device]
            table_ref[part] = table
            mine = w_ref[device].astype(jnp.float32)
            lane = lax.broadcasted_iota(jnp.int32, mine.shape, 1)
            query = jnp.where(lane < 64, 0.0, pltpu.roll(mine, 64, 1)).astype(jnp.bfloat16)
            scores = lax.dot_general(
                table, query, (((1,), (1,)), ((), ())), preferred_element_type=jnp.float32
            )
            place = lax.broadcasted_iota(jnp.int32, scores.shape, 0)
            for k in range(t_ref.shape[1]):
                hit = place == slot_ref[part, k : k + 1, :]
                t_ref[part, k : k + 1, :] = jnp.sum(jnp.where(hit, scores, 0.0), axis=0, keepdims=True)


def neg_forward(hot, w, slots):
    peers, places, rows = hot.shape
    neg = slots.shape[1]
    half = peers // 2
    late = lambda i: (jnp.maximum(i - half, 0), 0, 0)
    return pl.pallas_call(
        functools.partial(neg_forward_kernel, half),
        grid=(2 * half,),
        in_specs=[
            pl.BlockSpec((2, places, rows), lambda i: (jnp.minimum(i, half - 1), 0, 0)),
            pl.BlockSpec((peers, rows, 128), lambda i: (0, 0, 0)),
            pl.BlockSpec((2, neg, rows), late),
        ],
        out_specs=[pl.BlockSpec((2, neg, rows), late), pl.BlockSpec((2, places, 128), late)],
        out_shape=[
            jax.ShapeDtypeStruct((peers, neg, rows), jnp.float32),
            jax.ShapeDtypeStruct((peers, places, 128), jnp.bfloat16),
        ],
        scratch_shapes=[pltpu.VMEM((peers, places, 128), jnp.bfloat16)],
        compiler_params=pltpu.CompilerParams(vmem_limit_bytes=32 * MIB),
        cost_estimate=pl.CostEstimate(
            flops=4 * peers * places * rows * 128, bytes_accessed=20 * MIB, transcendentals=0
        ),
        name="neg_forward",
    )(hot, w, slots)


def neg_backward_kernel(half, table_ref, w_ref, slot_ref, v_ref, ask_ref, y_ref, sums, q_part):
    step = pl.program_id(0)
    rows = w_ref.shape[1]
    places = table_ref.shape[1]

    @pl.when(step < half)
    def _():
        grads = []
        for part in range(2):
            device = 2 * step + part
            place = lax.broadcasted_iota(jnp.int32, (places, rows), 0)
            weight = jnp.zeros((places, rows), jnp.float32)
            for k in range(slot_ref.shape[1]):
                hit = place == slot_ref[part, k : k + 1, :]
                weight = weight + jnp.where(hit, v_ref[part, k : k + 1, :], 0.0)
            weight = weight.astype(jnp.bfloat16)
            q_part[device] = lax.dot_general(
                weight, table_ref[part], (((0,), (0,)), ((), ())), preferred_element_type=jnp.float32
            )
            rows_back = jnp.dot(weight, w_ref[device], preferred_element_type=jnp.float32) / TEMP
            grads.append(rows_back.reshape(-1, SLOTS, 128))
        both = jnp.concatenate(grads, axis=1).astype(jnp.bfloat16)
        sums[:, pl.ds(pl.multiple_of(step * 16, 16), 16), :] = both

    @pl.when(step >= half)
    def _():
        for part in range(2):
            owner = 2 * (step - half) + part
            target = lax.broadcasted_iota(jnp.int32, (rows, places), 0)
            hot = jnp.where(target == ask_ref[part], 1.0, 0.0).astype(jnp.bfloat16)
            p_grad = jnp.dot(hot, sums[owner], preferred_element_type=jnp.float32)
            lane = lax.broadcasted_iota(jnp.int32, p_grad.shape, 1)
            y_ref[part] = jnp.where(lane < 64, p_grad, q_part[owner] / TEMP).astype(jnp.bfloat16)


def neg_backward(table, w, slots, v, asked):
    peers, places, _ = table.shape
    rows = w.shape[1]
    neg = slots.shape[1]
    half = peers // 2
    early = lambda i: (jnp.minimum(i, half - 1), 0, 0)
    late = lambda i: (jnp.maximum(i - half, 0), 0, 0)
    return pl.pallas_call(
        functools.partial(neg_backward_kernel, half),
        grid=(2 * half,),
        in_specs=[
            pl.BlockSpec((2, places, 128), early),
            pl.BlockSpec((peers, rows, 128), lambda i: (0, 0, 0)),
            pl.BlockSpec((2, neg, rows), early),
            pl.BlockSpec((2, neg, rows), early),
            pl.BlockSpec((2, 1, places), late),
        ],
        out_specs=pl.BlockSpec((2, rows, 128), late),
        out_shape=jax.ShapeDtypeStruct((peers, rows, 128), jnp.bfloat16),
        scratch_shapes=[
            pltpu.VMEM((peers, places, 128), jnp.bfloat16),
            pltpu.VMEM((peers, rows, 128), jnp.float32),
        ],
        compiler_params=pltpu.CompilerParams(vmem_limit_bytes=40 * MIB),
        cost_estimate=pl.CostEstimate(
            flops=6 * peers * places * rows * 128, bytes_accessed=14 * MIB, transcendentals=0
        ),
        name="neg_backward",
    )(table, w, slots, v, asked)


def window_kernel(w_ref, z_ref, *refs):
    q_refs, p_refs, (q_out, p_out) = refs[:STOPS], refs[STOPS : 2 * STOPS], refs[2 * STOPS :]
    rows = w_ref.shape[0]
    q_grad = jnp.zeros(q_out.shape, jnp.float32)
    p_grad = jnp.zeros(p_out.shape, jnp.float32)
    for stop in range(STOPS):
        weight = w_ref[:, stop * rows : (stop + 1) * rows]
        q_grad = q_grad + jnp.dot(weight, p_refs[stop][...], preferred_element_type=jnp.float32)
        p_grad = p_grad + lax.dot_general(
            z_ref[stop], q_refs[stop][...], (((0,), (0,)), ((), ())), preferred_element_type=jnp.float32
        )
    q_out[...] = q_grad / TEMP
    p_out[...] = p_grad / TEMP


def window_grads(weight, back, q_blocks, p_blocks):
    rows, width = q_blocks[0].shape
    step = 512
    tile = pl.BlockSpec((rows, step), lambda i: (0, i))
    return pl.pallas_call(
        window_kernel,
        grid=(width // step,),
        in_specs=[
            pl.BlockSpec((rows, STOPS * rows), lambda i: (0, 0)),
            pl.BlockSpec((STOPS, rows, rows), lambda i: (0, 0, 0)),
        ]
        + [tile] * (2 * STOPS),
        out_specs=[tile, tile],
        out_shape=[jax.ShapeDtypeStruct((rows, width), jnp.float32)] * 2,
        compiler_params=pltpu.CompilerParams(vmem_limit_bytes=32 * MIB),
        cost_estimate=pl.CostEstimate(
            flops=4 * STOPS * rows * rows * width, bytes_accessed=12 * MIB, transcendentals=0
        ),
        name="window_grads",
    )(weight, back, *q_blocks, *p_blocks)


def final_kernel(q_ref, p_ref, gain_ref, qn_ref, pn_ref, qg_ref, pg_ref, y_ref, q_out, p_out, gain_out, q_all, p_all):
    width = q_ref.shape[1]
    low = lax.broadcasted_iota(jnp.int32, (q_ref.shape[0], 128), 1) < 64
    for tile in range(width // 128):
        cut = slice(tile * 128, (tile + 1) * 128)
        even = y_ref[2 * tile].astype(jnp.float32)
        odd = y_ref[2 * tile + 1].astype(jnp.float32)
        p_all[:, cut] = pg_ref[:, cut] + jnp.where(low, even, pltpu.roll(odd, 64, 1))
        q_all[:, cut] = qg_ref[:, cut] + jnp.where(low, pltpu.roll(even, 64, 1), odd)
    gain = gain_ref[...]
    total = jnp.zeros((1, width), jnp.float32)
    for src, norm, grads, out in ((q_ref, qn_ref, q_all, q_out), (p_ref, pn_ref, p_all, p_out)):
        hidden = src[...].astype(jnp.float32)
        inverse = 1.0 / norm[:, :1]
        unit = hidden * gain * inverse
        grad = grads[...]
        inner = jnp.sum(unit * grad, axis=-1, keepdims=True)
        scaled = (grad - unit * inner) * inverse
        out[...] = scaled * gain
        total = total + jnp.sum(hidden * scaled, axis=0, keepdims=True)

    @pl.when(pl.program_id(0) == 0)
    def _():
        gain_out[...] = jnp.zeros_like(gain_out)

    gain_out[...] += total


def finish(q_hidden, p_hidden, gain, q_norm, p_norm, q_grad, p_grad, y):
    rows, width = q_hidden.shape
    step = 32
    row_block = pl.BlockSpec((step, width), lambda i: (i, 0))
    norm_block = pl.BlockSpec((step, 128), lambda i: (i, 0))
    gain_block = pl.BlockSpec((1, width), lambda i: (0, 0))
    return pl.pallas_call(
        final_kernel,
        grid=(rows // step,),
        in_specs=[
            row_block,
            row_block,
            gain_block,
            norm_block,
            norm_block,
            row_block,
            row_block,
            pl.BlockSpec((width // 64, step, 128), lambda i: (0, i, 0)),
        ],
        out_specs=[row_block, row_block, gain_block],
        out_shape=[
            jax.ShapeDtypeStruct((rows, width), jnp.float32),
            jax.ShapeDtypeStruct((rows, width), jnp.float32),
            jax.ShapeDtypeStruct((1, width), jnp.float32),
        ],
        scratch_shapes=[pltpu.VMEM((step, width), jnp.float32)] * 2,
        compiler_params=pltpu.CompilerParams(vmem_limit_bytes=40 * MIB),
        cost_estimate=pl.CostEstimate(flops=20 * rows * width, bytes_accessed=24 * rows * width, transcendentals=0),
        name="finish",
    )(q_hidden, p_hidden, gain.reshape(1, width), q_norm, p_norm, q_grad, p_grad, y)


def slot_tables(wanted, peers):
    rows, neg = wanted.shape
    flat = wanted.T.reshape(-1)
    count = flat.shape[0]
    owner = flat // rows
    place = jnp.arange(count, dtype=jnp.int32)
    same = flat[:, None] == flat[None, :]
    again = jnp.any(same & (place[None, :] < place[:, None]), axis=1)
    smaller = (owner[:, None] == owner[None, :]) & (flat[:, None] < flat[None, :])
    rank = jnp.sum((smaller & ~again[:, None]).astype(jnp.int32), axis=0)
    slot = owner * SLOTS + rank
    table = jnp.arange(peers * SLOTS, dtype=jnp.int32)
    hit = (slot[None, :] == table[:, None]) & ~again[None, :]
    named = jnp.sum(jnp.where(hit, flat[None, :] % rows + 1, 0), axis=1) - 1
    return slot, named


def local(query_hidden, passage_hidden, norm_gain, negatives):
    q_hidden, p_hidden, wanted = query_hidden[0], passage_hidden[0], negatives[0]
    rows, width = q_hidden.shape
    neg = wanted.shape[1]
    peers = lax.axis_size("batch")
    me = lax.axis_index("batch")

    q_emb, p_emb, tiles, q_norm, p_norm = normalize(q_hidden, p_hidden, norm_gain)
    w = lax.all_to_all(tiles, "batch", split_axis=0, concat_axis=0, tiled=True)

    slot, named = slot_tables(wanted, peers)
    tables = lax.all_gather(jnp.concatenate([named, slot]), "batch")
    named_all = tables[:, : peers * SLOTS].reshape(peers, peers, SLOTS)
    asked = named_all.transpose(1, 0, 2).reshape(peers, peers * SLOTS)
    slots = tables[:, peers * SLOTS :].reshape(peers, neg, rows)
    hot = (asked[:, :, None] == jnp.arange(rows, dtype=jnp.int32)).astype(jnp.bfloat16)

    p_blocks, q_blocks = [p_emb], [q_emb]
    for _ in range(1, STOPS):
        p_blocks.append(from_behind(p_blocks[-1], "batch", 1))
        q_blocks.append(from_behind(q_blocks[-1], "batch", -1))

    t_part, neg_table = neg_forward(hot, w, slots)
    t_parts = lax.all_to_all(t_part, "batch", split_axis=0, concat_axis=0, tiled=True)
    neg_scores = jnp.sum(t_parts, axis=0) / TEMP

    scores = jnp.concatenate(
        [jnp.dot(q_emb, block.T, preferred_element_type=jnp.float32) for block in p_blocks], axis=1
    ) / TEMP
    exp_scores = jnp.exp(scores)
    exp_negative = jnp.exp(neg_scores)
    partition = jnp.sum(exp_scores, axis=1) + jnp.sum(exp_negative, axis=0)
    inverse = 1.0 / partition
    query_loss = jnp.log(partition) - jnp.diagonal(scores[:, :rows])
    identity = jnp.eye(rows, STOPS * rows, dtype=jnp.float32)
    weight = (exp_scores * inverse[:, None] - identity).astype(jnp.bfloat16)
    neg_weight = (exp_negative * inverse[None, :]).astype(jnp.bfloat16).astype(jnp.float32)

    shared = lax.all_gather(jnp.concatenate([neg_weight, inverse[None, :]], axis=0), "batch")
    y = neg_backward(neg_table, w, slots, shared[:, :neg], asked[:, None, :])
    y_back = lax.all_to_all(y, "batch", split_axis=0, concat_axis=0, tiled=True)

    back = [weight[:, :rows]]
    for stop in range(1, STOPS):
        others = jnp.exp(jnp.dot(q_blocks[stop], p_emb.T, preferred_element_type=jnp.float32) / TEMP)
        their_inverse = lax.dynamic_index_in_dim(shared[:, neg], (me + stop) % peers, keepdims=False)
        back.append((others * their_inverse[:, None]).astype(jnp.bfloat16))
    q_grad, p_grad = window_grads(weight, jnp.stack(back), q_blocks, p_blocks)

    query_grad, passage_grad, gain_part = finish(
        q_hidden, p_hidden, norm_gain, q_norm, p_norm, q_grad, p_grad, y_back
    )
    gain_grad = lax.psum(gain_part[0], ("batch", "rep"))
    return (query_grad[None], passage_grad[None], query_loss[None], gain_grad)


def solution(mesh):
    return jax.shard_map(
        local,
        mesh=mesh,
        in_specs=(P("rep", "batch", None), P("rep", "batch", None), P(), P("rep", "batch", None)),
        out_specs=(P("rep", "batch", None), P("rep", "batch", None), P("rep", "batch"), P()),
        check_vma=False,
    )
```

time: 948 us -> 769 us (0.81)
  waiting for transfers between devices: 531 us -> 156 us
  blocking collectives: 78.6 us -> 443 us
  local copies, waits for them, and re-layouts: 223 us -> 34.4 us
  Pallas kernels: 0 us -> 63 us
  matrix products: 47.8 us -> 8.62 us
  starting transfers between devices: 37.9 us -> 53 us
  other arithmetic: 18.8 us -> 8.26 us
    all_gather x0 -> x2, blocking collectives: none -> 316 us  [the longest x1 167 us: local(): tables = lax.all_gather(jnp.concatenate([named, slot]), 'batch')]
    ppermute x6, waiting for transfers between devices: 372 us -> 148 us  [from_behind(): return lax.ppermute(block, axis, route)]
    all_to_all x3, waiting for transfers between devices: 159 us -> 8.39 us  [the longest x1 8.38 us: local(): lax.all_to_all(t_part, 'batch', split_axis=0, concat_axis=0, tiled=True)]
    scatter x3 -> x0, local copies, waits for them, and re-layouts: 132 us -> none  [the longest x2 112 us: local(): outgoing = jnp.zeros((peer_count, capacity, feat_width), jnp.bfloat16).at...]
    pallas_call x0 -> x5, Pallas kernels: none -> 63 us  [the longest x1 26.4 us: neg_forward(): pl.pallas_call(functools.partial(neg_forward_kernel, half), grid=(2 * hal...]
    psum x1, blocking collectives: 78.6 us -> 127 us  [local(): gain_grad = lax.psum(gain_part[0], ('batch', 'rep'))]
    dot_general x7, matrix products: 47.8 us -> 8.62 us  [the longest x4 4.83 us: local(): jnp.dot(q_emb, block.T, preferred_element_type=jnp.float32)]
    gather x4 -> x1, local copies, waits for them, and re-layouts: 34.9 us -> 1.25 us  [local(): query_loss = jnp.log(partition) - jnp.diagonal(scores[:, :rows])]
  transfers between devices with their start and end apart: 9 -> 9, of which waited for: 8 -> 5; matrix products, arithmetic and copies ran while one was open for 6% -> 3% of each run, Pallas kernels for 0% -> 4%
where the time goes in v1:
time: 769 us; the launch traced here: 767 us
  blocking collectives  443 us (58%)
  waiting for transfers between devices  156 us (20%)
  Pallas kernels  63 us (8%)
  starting transfers between devices  53 us (7%)
  local copies, waits for them, and re-layouts  34.4 us (4%)
  matrix products  8.62 us (1%)
  other arithmetic  8.26 us (1%)
    all_gather x1, blocking collectives, local(): tables = lax.all_gather(jnp.concatenate([named, slot]), 'batch')  167 us
    all_gather x1, blocking collectives, local(): lax.all_gather(jnp.concatenate([neg_weight, inverse[None, :]], axis=0), '...  149 us
    ppermute x6, waiting for transfers between devices, from_behind(): return lax.ppermute(block, axis, route)  148 us
    psum x1, blocking collectives, local(): gain_grad = lax.psum(gain_part[0], ('batch', 'rep'))  127 us
    pallas_call x1, Pallas kernels, neg_forward(): pl.pallas_call(functools.partial(neg_forward_kernel, half), grid=(2 * hal...  26.4 us
    unnamed x64, local copies, waits for them, and re-layouts  25.4 us
    ppermute x6, starting transfers between devices, from_behind(): return lax.ppermute(block, axis, route)  24.1 us
    pallas_call x1, Pallas kernels, neg_backward(): pl.pallas_call(functools.partial(neg_backward_kernel, half), grid=(2 * ha...  21.2 us
  transfers between devices with their start and end apart: 9, of which 5 were waited for; matrix products, arithmetic and copies ran while one was open for 3% of the time, Pallas kernels for 4%

profile of v1, /device:TPU:1, one launch (start us, length us, event | category | flops | bytes accessed | tf_op | source)
XLA Modules:
  0.0 767.3 jit_solution(422447975612894086)
XLA Ops:
  0.6 1.2 copy-done.6
  1.9 1.2 copy-done.8
  3.1 0.7 copy-done.19
  3.8 2.0 normalize.1
  5.8 1.3 copy-done.10
  8.4 15.5 %all-to-all-start = ((bf16[64,128,128]{2,1,0:T(8,128)(2,1)}), bf16[64,128,128]{2,1,0:T(8,128)(2,1)}, u32[]{:S(2)}, u32[]{:S(2)}) async-start(bf16[64,128,128]{2,1,0:T(8,128)(2,1)} %copy-done.10), calls=%async_computation | async-start | bytes 4194304 | tf_op jit(solution)/shard_map/all_to_all | solution.py:318
  23.9 1.0 collective-permute-start
  25.7 72.4 %collective-permute-done.refs_5_ = bf16[128,4096]{1,0:T(8,128)(2,1)S(1)} collective-permute-done((bf16[128,4096]{1,0:T(8,128)(2,1)S(1)}, bf16[128,4096]{1,0:T(8,128)(2,1)S(1)}, u32[]{:S(2)}, u32[]{:S(2)}) %collective-permute-start) | collective-permute-done | bytes 1048608 | tf_op jit(solution)/shard_map/ppermute | solution.py:20
  98.2 167.5 %all-gather.2 = s32[64,1,896]{2,1,0:T(1,128)S(1)} all-gather(s32[1,1,896]{2,1,0:T(1,128)S(1)} %reshape.198), channel_id=2, replica_groups=mesh['batch'=64,'rep'=4] {'batch'}, dimensions={0}, use_global_device_ids=true | all-gather | bytes 232960 | tf_op jit(solution)/shard_map/all_gather | solution.py:321
  265.7 1.1 copy.44
  266.7 1.7 slice_bitcast_fusion
  268.4 1.1 copy.45
  269.6 6.6 fusion.hot_ref
  276.3 1.8 collective-permute-start.2
  278.1 1.6 slice.29
  279.7 1.0 copy.54.slot_ref
  280.7 1.1 copy.49.ask_ref
  282.3 1.1 fusion.24
  283.3 1.7 fusion.25
  285.0 3.4 copy-done
  288.4 26.4 %neg_forward.1 = (f32[64,3,128]{2,1,0:T(4,128)}, bf16[64,512,128]{2,1,0:T(8,128)(2,1)S(1)}) custom-call(bf16[64,512,128]{2,1,0:T(8,128)(2,1)S(1)} %copy-done, bf16[64,128,128]{2,1,0:T(8,128)(2,1)} %all-to-all-done.w_ref, s32[64,3,128]{2,1,0:T(4,128)S(1)} %copy.54.slot_ref), custom_call_target="tpu_custom_call" | custom-call | flops 2147483648 | bytes 20971520 | tf_op jit(solution)/shard_map/neg_forward/pallas_call | solution.py:108
  314.9 3.3 copy-done.2
  318.1 7.9 %all-to-all-start.1 = ((f32[64,3,128]{2,1,0:T(4,128)}), f32[64,3,128]{2,1,0:T(4,128)S(1)}, u32[]{:S(2)}, u32[]{:S(2)}) async-start(f32[64,3,128]{2,1,0:T(4,128)} %get-tuple-element.21), calls=%async_computation.1 | async-start | bytes 262144 | tf_op jit(solution)/shard_map/all_to_all | solution.py:333
  326.0 1.7 fusion.26
  327.9 1.2 gather_fusion
  329.2 8.4 %all-to-all-done.1 = f32[64,3,128]{2,1,0:T(4,128)S(1)} async-done(((f32[64,3,128]{2,1,0:T(4,128)}), f32[64,3,128]{2,1,0:T(4,128)S(1)}, u32[]{:S(2)}, u32[]{:S(2)}) %all-to-all-start.1) | async-done | bytes 98336 | tf_op jit(solution)/shard_map/all_to_all | solution.py:333
  338.2 148.9 %all-gather.3 = f32[64,4,128]{2,1,0:T(4,128)S(1)} all-gather(f32[1,4,128]{2,1,0:T(4,128)S(1)} %maximum_bitcast_fusion), channel_id=3, replica_groups=mesh['batch'=64,'rep'=4] {'batch'}, dimensions={0}, use_global_device_ids=true | all-gather | bytes 133120 | tf_op jit(solution)/shard_map/all_gather | solution.py:348
  487.0 3.4 copy-done.3
  490.4 21.2 %neg_backward.1 = bf16[64,128,128]{2,1,0:T(8,128)(2,1)S(1)} custom-call(bf16[64,512,128]{2,1,0:T(8,128)(2,1)S(1)} %copy-done.3, bf16[64,128,128]{2,1,0:T(8,128)(2,1)} %all-to-all-done.w_ref, s32[64,3,128]{2,1,0:T(4,128)S(1)} %copy.54.slot_ref, f32[64,3,128]{2,1,0:T(4,128)S(1)} %bitcast.65, s32[64,1,512]{2,1,0:T(1,128)S(1)} %copy.49.ask_ref), custom_call_target="tpu_custom_call" | custom-call | flops 3221225472 | bytes 14680064 | tf_op jit(solution)/shard_map/neg_backward/pallas_call | solution.py:172
  511.7 1.3 copy-done.1
  513.0 5.6 all-to-all-start.2
  518.5 7.0 collective-permute-start.3
  525.6 28.2 %collective-permute-done.3.refs_1_ = bf16[128,4096]{1,0:T(8,128)(2,1)S(1)} collective-permute-done((bf16[128,4096]{1,0:T(8,128)(2,1)S(1)}, bf16[128,4096]{1,0:T(8,128)(2,1)S(1)}, u32[]{:S(2)}, u32[]{:S(2)}) %collective-permute-start.3) | collective-permute-done | bytes 1048608 | tf_op jit(solution)/shard_map/ppermute | solution.py:20
  553.8 6.5 collective-permute-start.4
  560.3 11.7 %collective-permute-done.4.refs_2_ = bf16[128,4096]{1,0:T(8,128)(2,1)} collective-permute-done((bf16[128,4096]{1,0:T(8,128)(2,1)S(1)}, bf16[128,4096]{1,0:T(8,128)(2,1)}, u32[]{:S(2)}, u32[]{:S(2)}) %collective-permute-start.4) | collective-permute-done | bytes 1048608 | tf_op jit(solution)/shard_map/ppermute | solution.py:20
  572.0 7.7 %collective-permute-start.5 = (bf16[128,4096]{1,0:T(8,128)(2,1)}, bf16[128,4096]{1,0:T(8,128)(2,1)}, u32[]{:S(2)}, u32[]{:S(2)}) collective-permute-start(bf16[128,4096]{1,0:T(8,128)(2,1)} %collective-permute-done.4.refs_2_), channel_id=1, source_target_pairs={{4,0},{8,4},{12,8},{16,12},{20,16},{24,20},{28,24},{32,28},{36,32}... | collective-permute-start | bytes 3145736 | tf_op jit(solution)/shard_map/ppermute | solution.py:20
  579.8 1.7 fusion.11
  582.0 35.2 %collective-permute-done.5.refs_3_ = bf16[128,4096]{1,0:T(8,128)(2,1)} collective-permute-done((bf16[128,4096]{1,0:T(8,128)(2,1)}, bf16[128,4096]{1,0:T(8,128)(2,1)}, u32[]{:S(2)}, u32[]{:S(2)}) %collective-permute-start.5) | collective-permute-done | bytes 1048608 | tf_op jit(solution)/shard_map/ppermute | solution.py:20
  617.2 1.7 fusion.10
  619.0 6.9 window_grads.1
  626.0 1.3 copy-done.11
  627.3 1.3 copy-done.13
  628.6 1.2 copy-done.7
  629.9 1.2 copy-done.9
  631.1 1.6 copy-done.12
  632.7 1.6 copy-done.14
  634.3 6.4 finish.1
  640.6 126.7 %psum.7 = f32[4096]{0:T(1024)} all-reduce(f32[4096]{0:T(1024)S(1)} %bitcast.68), channel_id=1, replica_groups=mesh['batch'=64,'rep'=4] {'batch','rep'}, use_global_device_ids=true, to_apply=%region_6.7 | all-reduce | flops 4096 | bytes 32768 | tf_op jit(solution)/shard_map/psum | solution.py:362
  (79 shorter events, 4.1 us)
Async XLA Ops:
  0.6 1.2 copy-start.6
  1.9 1.2 copy-start.8
  3.1 0.7 copy-start.19
  5.8 1.3 copy-start.10
  7.2 0.6 copy-start.15
  7.8 0.6 copy-start.17
  8.4 16.5 %copy-start.30 = (s32[1,128,3]{1,0,2:T(1,128)S(1)}, s32[1,128,3]{1,0,2:T(1,128)}, u32[]{:S(2)}) copy-start(s32[1,128,3]{1,0,2:T(1,128)} %param.7) | copy-start | bytes 4612
  8.4 276.6 %all-to-all-start = ((bf16[64,128,128]{2,1,0:T(8,128)(2,1)}), bf16[64,128,128]{2,1,0:T(8,128)(2,1)}, u32[]{:S(2)}, u32[]{:S(2)}) async-start(bf16[64,128,128]{2,1,0:T(8,128)(2,1)} %copy-done.10), calls=%async_computation | async-start | bytes 4194304 | tf_op jit(solution)/shard_map/all_to_all | solution.py:318
  23.9 74.2 %collective-permute-start = (bf16[128,4096]{1,0:T(8,128)(2,1)S(1)}, bf16[128,4096]{1,0:T(8,128)(2,1)S(1)}, u32[]{:S(2)}, u32[]{:S(2)}) collective-permute-start(bf16[128,4096]{1,0:T(8,128)(2,1)S(1)} %get-tuple-element.19.refs_4_), channel_id=1, source_target_pairs={{252,0},{0,4},{4,8},{8,12},{12,16},{16,20},{20,24},{24,28},{28,32}... | collective-permute-start | bytes 3145736 | tf_op jit(solution)/shard_map/ppermute | solution.py:20
  98.2 184.1 %copy-start.4 = (bf16[128,4096]{1,0:T(8,128)(2,1)}, bf16[128,4096]{1,0:T(8,128)(2,1)S(1)}, u32[]{:S(2)}) copy-start(bf16[128,4096]{1,0:T(8,128)(2,1)S(1)} %collective-permute-done.refs_5_) | copy-start | bytes 3145732
  98.2 178.1 %collective-permute-start.1 = (bf16[128,4096]{1,0:T(8,128)(2,1)S(1)}, bf16[128,4096]{1,0:T(8,128)(2,1)}, u32[]{:S(2)}, u32[]{:S(2)}) collective-permute-start(bf16[128,4096]{1,0:T(8,128)(2,1)S(1)} %collective-permute-done.refs_5_), channel_id=1, source_target_pairs={{252,0},{0,4},{4,8},{8,12},{12,16},{16,20},{20,24},{24,28},{28,32}... | collective-permute-start | bytes 3145736 | tf_op jit(solution)/shard_map/ppermute | solution.py:20
  269.5 6.8 copy-start.21
  276.3 49.8 %collective-permute-start.2 = (bf16[128,4096]{1,0:T(8,128)(2,1)}, bf16[128,4096]{1,0:T(8,128)(2,1)}, u32[]{:S(2)}, u32[]{:S(2)}) collective-permute-start(bf16[128,4096]{1,0:T(8,128)(2,1)} %collective-permute-done.1.refs_6_), channel_id=1, source_target_pairs={{252,0},{0,4},{4,8},{8,12},{12,16},{16,20},{20,24},{24,28},{28,32}... | collective-permute-start | bytes 3145736 | tf_op jit(solution)/shard_map/ppermute | solution.py:20
  282.2 45.5 %copy-start.22 = (f32[128,128]{1,0:T(8,128)}, f32[128,128]{1,0:T(8,128)S(1)}, u32[]{:S(2)}) copy-start(f32[128,128]{1,0:T(8,128)S(1)} %fusion.23) | copy-start | bytes 196612
  285.0 42.7 %copy-start.26 = (f32[128,128]{1,0:T(8,128)}, f32[128,128]{1,0:T(8,128)S(1)}, u32[]{:S(2)}) copy-start(f32[128,128]{1,0:T(8,128)S(1)} %fusion.25) | copy-start | bytes 196612
  285.0 3.4 copy-start
  314.9 3.3 copy-start.2
  318.1 9.6 %copy-start.24 = (f32[128,128]{1,0:T(8,128)S(1)}, f32[128,128]{1,0:T(8,128)}, u32[]{:S(2)}) copy-start(f32[128,128]{1,0:T(8,128)} %fusion.24) | copy-start | bytes 196612
  318.1 19.4 %all-to-all-start.1 = ((f32[64,3,128]{2,1,0:T(4,128)}), f32[64,3,128]{2,1,0:T(4,128)S(1)}, u32[]{:S(2)}, u32[]{:S(2)}) async-start(f32[64,3,128]{2,1,0:T(4,128)} %get-tuple-element.21), calls=%async_computation.1 | async-start | bytes 262144 | tf_op jit(solution)/shard_map/all_to_all | solution.py:333
  327.7 183.9 %copy-start.28 = (f32[128,128]{1,0:T(8,128)}, f32[128,128]{1,0:T(8,128)S(1)}, u32[]{:S(2)}) copy-start(f32[128,128]{1,0:T(8,128)S(1)} %fusion.26) | copy-start | bytes 196612
  487.0 3.4 copy-start.3
  511.7 1.3 copy-start.1
  513.0 115.6 %all-to-all-start.2 = ((bf16[64,128,128]{2,1,0:T(8,128)(2,1)}), bf16[64,128,128]{2,1,0:T(8,128)(2,1)}, u32[]{:S(2)}, u32[]{:S(2)}) async-start(bf16[64,128,128]{2,1,0:T(8,128)(2,1)} %copy-done.1), calls=%async_computation.2 | async-start | bytes 4194304 | tf_op jit(solution)/shard_map/all_to_all | solution.py:350
  518.5 35.2 %collective-permute-start.3 = (bf16[128,4096]{1,0:T(8,128)(2,1)S(1)}, bf16[128,4096]{1,0:T(8,128)(2,1)S(1)}, u32[]{:S(2)}, u32[]{:S(2)}) collective-permute-start(bf16[128,4096]{1,0:T(8,128)(2,1)S(1)} %get-tuple-element.18.refs_0_), channel_id=1, source_target_pairs={{4,0},{8,4},{12,8},{16,12},{20,16},{24,20},{28,24},{32,28},{36,32}... | collective-permute-start | bytes 3145736 | tf_op jit(solution)/shard_map/ppermute | solution.py:20
  553.8 18.2 %collective-permute-start.4 = (bf16[128,4096]{1,0:T(8,128)(2,1)S(1)}, bf16[128,4096]{1,0:T(8,128)(2,1)}, u32[]{:S(2)}, u32[]{:S(2)}) collective-permute-start(bf16[128,4096]{1,0:T(8,128)(2,1)S(1)} %collective-permute-done.3.refs_1_), channel_id=1, source_target_pairs={{4,0},{8,4},{12,8},{16,12},{20,16},{24,20},{28,24},{32,28},{36,32}... | collective-permute-start | bytes 3145736 | tf_op jit(solution)/shard_map/ppermute | solution.py:20
  572.0 45.1 %collective-permute-start.5 = (bf16[128,4096]{1,0:T(8,128)(2,1)}, bf16[128,4096]{1,0:T(8,128)(2,1)}, u32[]{:S(2)}, u32[]{:S(2)}) collective-permute-start(bf16[128,4096]{1,0:T(8,128)(2,1)} %collective-permute-done.4.refs_2_), channel_id=1, source_target_pairs={{4,0},{8,4},{12,8},{16,12},{20,16},{24,20},{28,24},{32,28},{36,32}... | collective-permute-start | bytes 3145736 | tf_op jit(solution)/shard_map/ppermute | solution.py:20
  581.5 37.3 %copy-start.23 = (f32[128,128]{1,0:T(8,128)S(1)}, f32[128,128]{1,0:T(8,128)}, u32[]{:S(2)}) copy-start(f32[128,128]{1,0:T(8,128)} %copy-done.22) | copy-start | bytes 196612
  581.5 37.3 %copy-start.25 = (f32[128,128]{1,0:T(8,128)S(1)}, f32[128,128]{1,0:T(8,128)}, u32[]{:S(2)}) copy-start(f32[128,128]{1,0:T(8,128)} %fusion.24) | copy-start | bytes 196612
  581.5 37.3 %copy-start.27 = (f32[128,128]{1,0:T(8,128)S(1)}, f32[128,128]{1,0:T(8,128)}, u32[]{:S(2)}) copy-start(f32[128,128]{1,0:T(8,128)} %copy-done.26) | copy-start | bytes 196612
  581.5 37.3 %copy-start.29 = (f32[128,128]{1,0:T(8,128)S(1)}, f32[128,128]{1,0:T(8,128)}, u32[]{:S(2)}) copy-start(f32[128,128]{1,0:T(8,128)} %copy-done.28) | copy-start | bytes 196612
  581.5 37.5 %copy-start.5 = (bf16[128,4096]{1,0:T(8,128)(2,1)S(1)}, bf16[128,4096]{1,0:T(8,128)(2,1)}, u32[]{:S(2)}) copy-start(bf16[128,4096]{1,0:T(8,128)(2,1)} %copy-done.4) | copy-start | bytes 3145732
  619.0 9.6 %copy-start.16 = (f32[128,128]{1,0:T(8,128)S(1)}, f32[128,128]{1,0:T(8,128)}, u32[]{:S(2)}) copy-start(f32[128,128]{1,0:T(8,128)} %copy-done.15) | copy-start | bytes 196612
  619.0 9.6 %copy-start.18 = (f32[128,128]{1,0:T(8,128)S(1)}, f32[128,128]{1,0:T(8,128)}, u32[]{:S(2)}) copy-start(f32[128,128]{1,0:T(8,128)} %copy-done.17) | copy-start | bytes 196612
  619.0 9.6 %copy-start.20 = (f32[4096]{0:T(1024)S(1)}, f32[4096]{0:T(1024)}, u32[]{:S(2)}) copy-start(f32[4096]{0:T(1024)} %param.6) | copy-start | bytes 49156
  626.0 1.3 copy-start.11
  627.3 1.3 copy-start.13
  628.6 1.2 copy-start.7
  629.9 1.2 copy-start.9
  631.1 1.6 copy-start.12
  632.7 1.6 copy-start.14

commit v2 on v1

--- a/solution.py
+++ b/solution.py
@@ -290,6 +290,91 @@
     )(q_hidden, p_hidden, gain.reshape(1, width), q_norm, p_norm, q_grad, p_grad, y)
 
 
+MESH = pl.DeviceIdType.MESH
+LINE = 8
+
+
+def rounds(me, rep, peers, reps):
+    z, line = lax.rem(me, LINE), me // LINE
+    return (
+        (z, LINE, lambda i: (line * LINE + i, rep)),
+        (line, peers // LINE, lambda i: (i * LINE + z, rep)),
+        (rep, reps, lambda i: (me, i)),
+    )
+
+
+def sum_kernel(peers, reps, part_ref, out_ref, slots, send_sems, recv_sems):
+    me, rep = lax.axis_index("batch"), lax.axis_index("rep")
+    plan = rounds(me, rep, peers, reps)
+    barrier = pltpu.get_barrier_semaphore()
+    total = 0
+    for here, size, target in plan:
+        for off in range(1, size):
+            pl.semaphore_signal(barrier, inc=1, device_id=target(lax.rem(here + off, size)), device_id_type=MESH)
+            total += 1
+    pl.semaphore_wait(barrier, total)
+    out_ref[...] = part_ref[...]
+    for turn, (here, size, target) in enumerate(plan):
+        slots[turn, here] = out_ref[...]
+        copies = []
+        for off in range(1, size):
+            copies.append(
+                pltpu.make_async_remote_copy(
+                    src_ref=slots.at[turn, here],
+                    dst_ref=slots.at[turn, here],
+                    send_sem=send_sems.at[turn, off],
+                    recv_sem=recv_sems.at[turn, here],
+                    device_id=target(lax.rem(here + off, size)),
+                    device_id_type=MESH,
+                )
+            )
+            copies[-1].start()
+        for off in range(1, size):
+            other = lax.rem(here + off, size)
+            pltpu.make_async_remote_copy(
+                src_ref=slots.at[turn, other],
+                dst_ref=slots.at[turn, other],
+                send_sem=send_sems.at[turn, off],
+                recv_sem=recv_sems.at[turn, other],
+                device_id=target(other),
+                device_id_type=MESH,
+            ).wait_recv()
+        total = slots[turn, 0]
+        for i in range(1, size):
+            total = total + slots[turn, i]
+        out_ref[...] = total
+        for copy in copies:
+            copy.wait_send()
+
+
+def sum_over_devices(part):
+    peers, reps = lax.axis_size("batch"), lax.axis_size("rep")
+    width = part.shape[-1]
+    shape = (width // 128, 128)
+    most = max(LINE, peers // LINE, reps)
+    out = pl.pallas_call(
+        functools.partial(sum_kernel, peers, reps),
+        in_specs=[pl.BlockSpec(memory_space=pltpu.VMEM)],
+        out_specs=pl.BlockSpec(memory_space=pltpu.VMEM),
+        out_shape=jax.ShapeDtypeStruct(shape, jnp.float32),
+        scratch_shapes=[
+            pltpu.VMEM((3, most) + shape, jnp.float32),
+            pltpu.SemaphoreType.DMA((3, most)),
+            pltpu.SemaphoreType.DMA((3, most)),
+        ],
+        compiler_params=pltpu.CompilerParams(collective_id=0, has_side_effects=True),
+        name="gain_sum",
+    )(part.reshape(shape))
+    return out.reshape(width)
+
+
+def to_all(part):
+    peers = lax.axis_size("batch")
+    return lax.all_to_all(
+        jnp.broadcast_to(part[None], (peers,) + part.shape), "batch", split_axis=0, concat_axis=0, tiled=True
+    )
+
+
 def slot_tables(wanted, peers):
     rows, neg = wanted.shape
     flat = wanted.T.reshape(-1)
@@ -318,7 +403,7 @@
     w = lax.all_to_all(tiles, "batch", split_axis=0, concat_axis=0, tiled=True)
 
     slot, named = slot_tables(wanted, peers)
-    tables = lax.all_gather(jnp.concatenate([named, slot]), "batch")
+    tables = to_all(jnp.concatenate([named, slot]))
     named_all = tables[:, : peers * SLOTS].reshape(peers, peers, SLOTS)
     asked = named_all.transpose(1, 0, 2).reshape(peers, peers * SLOTS)
     slots = tables[:, peers * SLOTS :].reshape(peers, neg, rows)
@@ -345,7 +430,7 @@
     weight = (exp_scores * inverse[:, None] - identity).astype(jnp.bfloat16)
     neg_weight = (exp_negative * inverse[None, :]).astype(jnp.bfloat16).astype(jnp.float32)
 
-    shared = lax.all_gather(jnp.concatenate([neg_weight, inverse[None, :]], axis=0), "batch")
+    shared = to_all(jnp.concatenate([neg_weight, inverse[None, :]], axis=0))
     y = neg_backward(neg_table, w, slots, shared[:, :neg], asked[:, None, :])
     y_back = lax.all_to_all(y, "batch", split_axis=0, concat_axis=0, tiled=True)
 
@@ -359,7 +444,7 @@
     query_grad, passage_grad, gain_part = finish(
         q_hidden, p_hidden, norm_gain, q_norm, p_norm, q_grad, p_grad, y_back
     )
-    gain_grad = lax.psum(gain_part[0], ("batch", "rep"))
+    gain_grad = sum_over_devices(gain_part)
     return (query_grad[None], passage_grad[None], query_loss[None], gain_grad)
 
 

time: 769 us -> 425 us (0.55)
  blocking collectives: 443 us -> 0 us
  waiting for transfers between devices: 156 us -> 213 us
  Pallas kernels: 63 us -> 88.2 us
  starting transfers between devices: 53 us -> 64.6 us
    all_gather x2 -> x0, blocking collectives: 316 us -> none  [the longest x1 167 us: local(): tables = lax.all_gather(jnp.concatenate([named, slot]), 'batch')]
    psum x1 -> x0, blocking collectives: 127 us -> none  [local(): gain_grad = lax.psum(gain_part[0], ('batch', 'rep'))]
    ppermute x6, waiting for transfers between devices: 148 us -> 187 us  [from_behind(): return lax.ppermute(block, axis, route)]
    pallas_call x0 -> x1, Pallas kernels: none -> 25.2 us  [sum_over_devices(): pl.pallas_call(functools.partial(sum_kernel, peers, reps), in_specs=[pl.B...]
    all_to_all x0 -> x2, starting transfers between devices: none -> 19.7 us  [to_all(): lax.all_to_all(jnp.broadcast_to(part[None], (peers,) + part.shape), 'batc...]
    all_to_all x0 -> x2, waiting for transfers between devices: none -> 17.3 us  [to_all(): lax.all_to_all(jnp.broadcast_to(part[None], (peers,) + part.shape), 'batc...]
    all_to_all x1, starting transfers between devices: 15.5 us -> 6.57 us  [local(): w = lax.all_to_all(tiles, 'batch', split_axis=0, concat_axis=0, tiled=True)]
    unnamed x64 -> x46, local copies, waits for them, and re-layouts: 25.4 us -> 27.4 us
  transfers between devices with their start and end apart: 9 -> 11, of which waited for: 5 -> 8; matrix products, arithmetic and copies ran while one was open for 3% -> 6% of each run, Pallas kernels for 4% -> 8%
where the time goes in v2:
time: 425 us; the launch traced here: 424 us
  waiting for transfers between devices  213 us (50%)
  Pallas kernels  88.2 us (21%)
  starting transfers between devices  64.6 us (15%)
  local copies, waits for them, and re-layouts  39.5 us (9%)
  other arithmetic  9.68 us (2%)
  matrix products  7.97 us (2%)
    ppermute x6, waiting for transfers between devices, from_behind(): return lax.ppermute(block, axis, route)  187 us
    unnamed x46, local copies, waits for them, and re-layouts  27.4 us
    pallas_call x1, Pallas kernels, neg_forward(): pl.pallas_call(functools.partial(neg_forward_kernel, half), grid=(2 * hal...  26.4 us
    pallas_call x1, Pallas kernels, sum_over_devices(): pl.pallas_call(functools.partial(sum_kernel, peers, reps), in_specs=[pl.B...  25.2 us
    ppermute x6, starting transfers between devices, from_behind(): return lax.ppermute(block, axis, route)  22.9 us
    pallas_call x1, Pallas kernels, neg_backward(): pl.pallas_call(functools.partial(neg_backward_kernel, half), grid=(2 * ha...  21.2 us
    all_to_all x2, starting transfers between devices, to_all(): lax.all_to_all(jnp.broadcast_to(part[None], (peers,) + part.shape), 'batc...  19.7 us
    all_to_all x2, waiting for transfers between devices, to_all(): lax.all_to_all(jnp.broadcast_to(part[None], (peers,) + part.shape), 'batc...  17.3 us
  transfers between devices with their start and end apart: 11, of which 8 were waited for; matrix products, arithmetic and copies ran while one was open for 6% of the time, Pallas kernels for 8%

profile of v2, /device:TPU:1, one launch (start us, length us, event | category | flops | bytes accessed | tf_op | source)
XLA Modules:
  0.0 423.7 jit_solution(5186910771636985534)
XLA Ops:
  3.6 15.1 %all-to-all-start = ((s32[64,1,896]{2,1,0:T(1,128)}), s32[64,1,896]{2,1,0:T(1,128)S(1)}, u32[]{:S(2)}, u32[]{:S(2)}) async-start(s32[64,1,896]{2,1,0:T(1,128)} %broadcast_in_dim.26), calls=%async_computation | async-start | bytes 458752 | tf_op jit(solution)/shard_map/all_to_all | solution.py:373
  18.7 1.2 copy-done.6
  19.9 1.2 copy-done.8
  21.9 2.0 normalize.1
  23.9 1.3 copy-done.10
  25.2 5.9 %all-to-all-done = s32[64,1,896]{2,1,0:T(1,128)S(1)} async-done(((s32[64,1,896]{2,1,0:T(1,128)}), s32[64,1,896]{2,1,0:T(1,128)S(1)}, u32[]{:S(2)}, u32[]{:S(2)}) %all-to-all-start) | async-done | bytes 229408 | tf_op jit(solution)/shard_map/all_to_all | solution.py:373
  31.8 6.6 %all-to-all-start.1 = ((bf16[64,128,128]{2,1,0:T(8,128)(2,1)}), bf16[64,128,128]{2,1,0:T(8,128)(2,1)}, u32[]{:S(2)}, u32[]{:S(2)}) async-start(bf16[64,128,128]{2,1,0:T(8,128)(2,1)} %copy-done.10), calls=%async_computation.1 | async-start | bytes 4194304 | tf_op jit(solution)/shard_map/all_to_all | solution.py:403
  39.4 72.6 %collective-permute-done.refs_5_ = bf16[128,4096]{1,0:T(8,128)(2,1)S(1)} collective-permute-done((bf16[128,4096]{1,0:T(8,128)(2,1)S(1)}, bf16[128,4096]{1,0:T(8,128)(2,1)S(1)}, u32[]{:S(2)}, u32[]{:S(2)}) %collective-permute-start) | collective-permute-done | bytes 1048608 | tf_op jit(solution)/shard_map/ppermute | solution.py:20
  112.5 2.0 copy.35
  114.5 1.7 slice_bitcast_fusion
  116.1 1.8 copy.36
  117.9 1.1 copy.37
  119.0 21.4 %collective-permute-done.1.refs_6_ = bf16[128,4096]{1,0:T(8,128)(2,1)} collective-permute-done((bf16[128,4096]{1,0:T(8,128)(2,1)S(1)}, bf16[128,4096]{1,0:T(8,128)(2,1)}, u32[]{:S(2)}, u32[]{:S(2)}) %collective-permute-start.1) | collective-permute-done | bytes 1048608 | tf_op jit(solution)/shard_map/ppermute | solution.py:20
  140.4 6.5 %fusion.hot_ref = bf16[64,512,128]{2,1,0:T(8,128)(2,1)} fusion(s32[64,512]{1,0:T(8,128)S(1)} %copy.37), kind=kLoop, calls=%fused_computation.2 | loop fusion | flops 8388608 | bytes 8519680 | tf_op jit(solution)/shard_map/convert_element_type | solution.py:410
  146.9 1.6 slice.29
  148.6 1.0 copy.45.slot_ref
  150.1 1.7 fusion.25
  151.8 3.4 copy-done
  155.2 26.4 %neg_forward.1 = (f32[64,3,128]{2,1,0:T(4,128)}, bf16[64,512,128]{2,1,0:T(8,128)(2,1)S(1)}) custom-call(bf16[64,512,128]{2,1,0:T(8,128)(2,1)S(1)} %copy-done, bf16[64,128,128]{2,1,0:T(8,128)(2,1)} %all-to-all-done.1.w_ref, s32[64,3,128]{2,1,0:T(4,128)S(1)} %copy.45.slot_ref), custom_call_target="tpu_custom_call" | custom-call | flops 2147483648 | bytes 20971520 | tf_op jit(solution)/shard_map/neg_forward/pallas_call | solution.py:108
  181.6 3.3 copy-done.2
  184.9 9.6 %all-to-all-start.2 = ((f32[64,3,128]{2,1,0:T(4,128)}), f32[64,3,128]{2,1,0:T(4,128)S(1)}, u32[]{:S(2)}, u32[]{:S(2)}) async-start(f32[64,3,128]{2,1,0:T(4,128)} %get-tuple-element.21), calls=%async_computation.2 | async-start | bytes 262144 | tf_op jit(solution)/shard_map/all_to_all | solution.py:418
  194.5 1.7 fusion.26
  196.3 1.2 gather_fusion
  197.6 8.4 %all-to-all-done.2 = f32[64,3,128]{2,1,0:T(4,128)S(1)} async-done(((f32[64,3,128]{2,1,0:T(4,128)}), f32[64,3,128]{2,1,0:T(4,128)S(1)}, u32[]{:S(2)}, u32[]{:S(2)}) %all-to-all-start.2) | async-done | bytes 98336 | tf_op jit(solution)/shard_map/all_to_all | solution.py:418
  207.3 4.6 %all-to-all-start.3 = ((f32[64,4,128]{2,1,0:T(4,128)}), f32[64,4,128]{2,1,0:T(4,128)S(1)}, u32[]{:S(2)}, u32[]{:S(2)}) async-start(f32[64,4,128]{2,1,0:T(4,128)} %broadcast_in_dim.27), calls=%async_computation.3 | async-start | bytes 262144 | tf_op jit(solution)/shard_map/all_to_all | solution.py:373
  212.1 11.4 %all-to-all-done.3 = f32[64,4,128]{2,1,0:T(4,128)S(1)} async-done(((f32[64,4,128]{2,1,0:T(4,128)}), f32[64,4,128]{2,1,0:T(4,128)S(1)}, u32[]{:S(2)}, u32[]{:S(2)}) %all-to-all-start.3) | async-done | bytes 131104 | tf_op jit(solution)/shard_map/all_to_all | solution.py:373
  223.4 3.4 copy-done.3
  226.8 21.2 %neg_backward.1 = bf16[64,128,128]{2,1,0:T(8,128)(2,1)S(1)} custom-call(bf16[64,512,128]{2,1,0:T(8,128)(2,1)S(1)} %copy-done.3, bf16[64,128,128]{2,1,0:T(8,128)(2,1)} %all-to-all-done.1.w_ref, s32[64,3,128]{2,1,0:T(4,128)S(1)} %copy.45.slot_ref, f32[64,3,128]{2,1,0:T(4,128)S(1)} %bitcast.64, s32[64,1,512]{2,1,0:T(1,128)S(1)} %copy.40.ask_ref), custom_call_target="tpu_custom_call" | custom-call | flops 3221225472 | bytes 14680064 | tf_op jit(solution)/shard_map/neg_backward/pallas_call | solution.py:172
  248.1 1.3 copy-done.1
  249.4 5.7 %all-to-all-start.4 = ((bf16[64,128,128]{2,1,0:T(8,128)(2,1)}), bf16[64,128,128]{2,1,0:T(8,128)(2,1)}, u32[]{:S(2)}, u32[]{:S(2)}) async-start(bf16[64,128,128]{2,1,0:T(8,128)(2,1)} %copy-done.1), calls=%async_computation.4 | async-start | bytes 4194304 | tf_op jit(solution)/shard_map/all_to_all | solution.py:435
  255.1 7.0 %collective-permute-start.3 = (bf16[128,4096]{1,0:T(8,128)(2,1)S(1)}, bf16[128,4096]{1,0:T(8,128)(2,1)S(1)}, u32[]{:S(2)}, u32[]{:S(2)}) collective-permute-start(bf16[128,4096]{1,0:T(8,128)(2,1)S(1)} %get-tuple-element.18.refs_0_), channel_id=1, source_target_pairs={{4,0},{8,4},{12,8},{16,12},{20,16},{24,20},{28,24},{32,28},{36,32}... | collective-permute-start | bytes 3145736 | tf_op jit(solution)/shard_map/ppermute | solution.py:20
  262.2 58.6 %collective-permute-done.3.refs_1_ = bf16[128,4096]{1,0:T(8,128)(2,1)S(1)} collective-permute-done((bf16[128,4096]{1,0:T(8,128)(2,1)S(1)}, bf16[128,4096]{1,0:T(8,128)(2,1)S(1)}, u32[]{:S(2)}, u32[]{:S(2)}) %collective-permute-start.3) | collective-permute-done | bytes 1048608 | tf_op jit(solution)/shard_map/ppermute | solution.py:20
  320.8 6.8 %collective-permute-start.4 = (bf16[128,4096]{1,0:T(8,128)(2,1)S(1)}, bf16[128,4096]{1,0:T(8,128)(2,1)}, u32[]{:S(2)}, u32[]{:S(2)}) collective-permute-start(bf16[128,4096]{1,0:T(8,128)(2,1)S(1)} %collective-permute-done.3.refs_1_), channel_id=1, source_target_pairs={{4,0},{8,4},{12,8},{16,12},{20,16},{24,20},{28,24},{32,28},{36,32}... | collective-permute-start | bytes 3145736 | tf_op jit(solution)/shard_map/ppermute | solution.py:20
  327.6 19.1 %collective-permute-done.4.refs_2_ = bf16[128,4096]{1,0:T(8,128)(2,1)} collective-permute-done((bf16[128,4096]{1,0:T(8,128)(2,1)S(1)}, bf16[128,4096]{1,0:T(8,128)(2,1)}, u32[]{:S(2)}, u32[]{:S(2)}) %collective-permute-start.4) | collective-permute-done | bytes 1048608 | tf_op jit(solution)/shard_map/ppermute | solution.py:20
  346.7 8.0 %collective-permute-start.5 = (bf16[128,4096]{1,0:T(8,128)(2,1)}, bf16[128,4096]{1,0:T(8,128)(2,1)}, u32[]{:S(2)}, u32[]{:S(2)}) collective-permute-start(bf16[128,4096]{1,0:T(8,128)(2,1)} %collective-permute-done.4.refs_2_), channel_id=1, source_target_pairs={{4,0},{8,4},{12,8},{16,12},{20,16},{24,20},{28,24},{32,28},{36,32}... | collective-permute-start | bytes 3145736 | tf_op jit(solution)/shard_map/ppermute | solution.py:20
  355.8 1.7 fusion.11
  357.9 15.3 %collective-permute-done.5.refs_3_ = bf16[128,4096]{1,0:T(8,128)(2,1)} collective-permute-done((bf16[128,4096]{1,0:T(8,128)(2,1)}, bf16[128,4096]{1,0:T(8,128)(2,1)}, u32[]{:S(2)}, u32[]{:S(2)}) %collective-permute-start.5) | collective-permute-done | bytes 1048608 | tf_op jit(solution)/shard_map/ppermute | solution.py:20
  373.2 1.7 fusion.10
  374.9 6.9 %window_grads.1 = (f32[128,4096]{1,0:T(8,128)S(1)}, f32[128,4096]{1,0:T(8,128)S(1)}) custom-call(bf16[128,512]{1,0:T(8,128)(2,1)S(1)} %subtract_convert_fusion.w_ref, bf16[4,128,128]{2,1,0:T(8,128)(2,1)S(1)} %pad_maximum_fusion.z_ref, bf16[128,4096]{1,0:T(8,128)(2,1)S(1)} %get-tuple-element.18.refs_0_, bf16[128,4096]{1,0:T(8,128)(2,1)S(1)} %collective-permute-done.3.refs_1_, ...), custom_call_target="tpu_custom_call" | custom-call | flops 1073741824 | bytes 12582912 | tf_op jit(solution)/shard_map/window_grads/pallas_call | solution.py:215
  381.9 1.3 copy-done.11
  383.2 1.3 copy-done.13
  384.5 1.2 copy-done.7
  385.8 1.2 copy-done.9
  387.0 1.6 copy-done.12
  388.6 1.6 copy-done.14
  390.2 6.4 %finish.1 = (f32[128,4096]{1,0:T(8,128)}, f32[128,4096]{1,0:T(8,128)}, f32[1,4096]{1,0:T(1,128)S(1)}) custom-call(bf16[128,4096]{1,0:T(8,128)(2,1)S(1)} %bitcast.61, bf16[128,4096]{1,0:T(8,128)(2,1)S(1)} %bitcast.63, f32[1,4096]{1,0:T(1,128)S(1)} %bitcast.66, f32[128,128]{1,0:T(8,128)S(1)} %get-tuple-element.16.qn_ref, ...), custom_call_target="tpu_custom_call" | custom-call | flops 10485760 | bytes 12582912 | tf_op jit(solution)/shard_map/finish/pallas_call | solution.py:267
  397.1 25.2 %gain_sum.1 = f32[32,128]{1,0:T(8,128)} custom-call(f32[32,128]{1,0:T(8,128)} %bitcast.67), custom_call_target="tpu_custom_call" | custom-call | tf_op jit(solution)/shard_map/gain_sum/pallas_call | solution.py:355
  422.4 1.3 copy.54
  (65 shorter events, 10.0 us)
Async XLA Ops:
  3.6 27.6 %all-to-all-start = ((s32[64,1,896]{2,1,0:T(1,128)}), s32[64,1,896]{2,1,0:T(1,128)S(1)}, u32[]{:S(2)}, u32[]{:S(2)}) async-start(s32[64,1,896]{2,1,0:T(1,128)} %broadcast_in_dim.26), calls=%async_computation | async-start | bytes 458752 | tf_op jit(solution)/shard_map/all_to_all | solution.py:373
  18.7 1.2 copy-start.6
  19.9 1.2 copy-start.8
  21.1 0.7 copy-start.15
  23.9 1.3 copy-start.10
  31.2 0.7 copy-start.19
  31.8 119.9 %all-to-all-start.1 = ((bf16[64,128,128]{2,1,0:T(8,128)(2,1)}), bf16[64,128,128]{2,1,0:T(8,128)(2,1)}, u32[]{:S(2)}, u32[]{:S(2)}) async-start(bf16[64,128,128]{2,1,0:T(8,128)(2,1)} %copy-done.10), calls=%async_computation.1 | async-start | bytes 4194304 | tf_op jit(solution)/shard_map/all_to_all | solution.py:403
  38.4 73.6 %collective-permute-start = (bf16[128,4096]{1,0:T(8,128)(2,1)S(1)}, bf16[128,4096]{1,0:T(8,128)(2,1)S(1)}, u32[]{:S(2)}, u32[]{:S(2)}) collective-permute-start(bf16[128,4096]{1,0:T(8,128)(2,1)S(1)} %get-tuple-element.19.refs_4_), channel_id=1, source_target_pairs={{252,0},{0,4},{4,8},{8,12},{12,16},{16,20},{20,24},{24,28},{28,32}... | collective-permute-start | bytes 3145736 | tf_op jit(solution)/shard_map/ppermute | solution.py:20
  112.1 37.6 %copy-start.4 = (bf16[128,4096]{1,0:T(8,128)(2,1)}, bf16[128,4096]{1,0:T(8,128)(2,1)S(1)}, u32[]{:S(2)}) copy-start(bf16[128,4096]{1,0:T(8,128)(2,1)S(1)} %collective-permute-done.refs_5_) | copy-start | bytes 3145732
  112.1 28.4 %collective-permute-start.1 = (bf16[128,4096]{1,0:T(8,128)(2,1)S(1)}, bf16[128,4096]{1,0:T(8,128)(2,1)}, u32[]{:S(2)}, u32[]{:S(2)}) collective-permute-start(bf16[128,4096]{1,0:T(8,128)(2,1)S(1)} %collective-permute-done.refs_5_), channel_id=1, source_target_pairs={{252,0},{0,4},{4,8},{8,12},{12,16},{16,20},{20,24},{24,28},{28,32}... | collective-permute-start | bytes 3145736 | tf_op jit(solution)/shard_map/ppermute | solution.py:20
  140.4 54.0 %collective-permute-start.2 = (bf16[128,4096]{1,0:T(8,128)(2,1)}, bf16[128,4096]{1,0:T(8,128)(2,1)}, u32[]{:S(2)}, u32[]{:S(2)}) collective-permute-start(bf16[128,4096]{1,0:T(8,128)(2,1)} %collective-permute-done.1.refs_6_), channel_id=1, source_target_pairs={{252,0},{0,4},{4,8},{8,12},{12,16},{16,20},{20,24},{24,28},{28,32}... | collective-permute-start | bytes 3145736 | tf_op jit(solution)/shard_map/ppermute | solution.py:20
  151.7 44.4 %copy-start.20 = (f32[128,128]{1,0:T(8,128)}, f32[128,128]{1,0:T(8,128)S(1)}, u32[]{:S(2)}) copy-start(f32[128,128]{1,0:T(8,128)S(1)} %fusion.25) | copy-start | bytes 196612
  151.7 3.4 copy-start
  181.6 3.3 copy-start.2
  184.9 27.1 %copy-start.18 = (s32[64,64,8]{0,2,1:T(8,128)S(1)}, s32[64,64,8]{0,2,1:T(8,128)}, u32[]{:S(2)}) copy-start(s32[64,64,8]{0,2,1:T(8,128)} %copy.36) | copy-start | bytes 393220
  184.9 21.1 %all-to-all-start.2 = ((f32[64,3,128]{2,1,0:T(4,128)}), f32[64,3,128]{2,1,0:T(4,128)S(1)}, u32[]{:S(2)}, u32[]{:S(2)}) async-start(f32[64,3,128]{2,1,0:T(4,128)} %get-tuple-element.21), calls=%async_computation.2 | async-start | bytes 262144 | tf_op jit(solution)/shard_map/all_to_all | solution.py:418
  196.2 15.8 %copy-start.21 = (f32[128,128]{1,0:T(8,128)}, f32[128,128]{1,0:T(8,128)S(1)}, u32[]{:S(2)}) copy-start(f32[128,128]{1,0:T(8,128)S(1)} %fusion.26) | copy-start | bytes 196612
  207.3 16.1 %all-to-all-start.3 = ((f32[64,4,128]{2,1,0:T(4,128)}), f32[64,4,128]{2,1,0:T(4,128)S(1)}, u32[]{:S(2)}, u32[]{:S(2)}) async-start(f32[64,4,128]{2,1,0:T(4,128)} %broadcast_in_dim.27), calls=%async_computation.3 | async-start | bytes 262144 | tf_op jit(solution)/shard_map/all_to_all | solution.py:373
  223.4 3.4 copy-start.3
  248.1 1.3 copy-start.1
  249.4 135.1 %all-to-all-start.4 = ((bf16[64,128,128]{2,1,0:T(8,128)(2,1)}), bf16[64,128,128]{2,1,0:T(8,128)(2,1)}, u32[]{:S(2)}, u32[]{:S(2)}) async-start(bf16[64,128,128]{2,1,0:T(8,128)(2,1)} %copy-done.1), calls=%async_computation.4 | async-start | bytes 4194304 | tf_op jit(solution)/shard_map/all_to_all | solution.py:435
  255.1 65.7 %collective-permute-start.3 = (bf16[128,4096]{1,0:T(8,128)(2,1)S(1)}, bf16[128,4096]{1,0:T(8,128)(2,1)S(1)}, u32[]{:S(2)}, u32[]{:S(2)}) collective-permute-start(bf16[128,4096]{1,0:T(8,128)(2,1)S(1)} %get-tuple-element.18.refs_0_), channel_id=1, source_target_pairs={{4,0},{8,4},{12,8},{16,12},{20,16},{24,20},{28,24},{32,28},{36,32}... | collective-permute-start | bytes 3145736 | tf_op jit(solution)/shard_map/ppermute | solution.py:20
  320.8 25.9 %collective-permute-start.4 = (bf16[128,4096]{1,0:T(8,128)(2,1)S(1)}, bf16[128,4096]{1,0:T(8,128)(2,1)}, u32[]{:S(2)}, u32[]{:S(2)}) collective-permute-start(bf16[128,4096]{1,0:T(8,128)(2,1)S(1)} %collective-permute-done.3.refs_1_), channel_id=1, source_target_pairs={{4,0},{8,4},{12,8},{16,12},{20,16},{24,20},{28,24},{32,28},{36,32}... | collective-permute-start | bytes 3145736 | tf_op jit(solution)/shard_map/ppermute | solution.py:20
  346.7 26.5 %collective-permute-start.5 = (bf16[128,4096]{1,0:T(8,128)(2,1)}, bf16[128,4096]{1,0:T(8,128)(2,1)}, u32[]{:S(2)}, u32[]{:S(2)}) collective-permute-start(bf16[128,4096]{1,0:T(8,128)(2,1)} %collective-permute-done.4.refs_2_), channel_id=1, source_target_pairs={{4,0},{8,4},{12,8},{16,12},{20,16},{24,20},{28,24},{32,28},{36,32}... | collective-permute-start | bytes 3145736 | tf_op jit(solution)/shard_map/ppermute | solution.py:20
  357.5 17.5 %copy-start.5 = (bf16[128,4096]{1,0:T(8,128)(2,1)S(1)}, bf16[128,4096]{1,0:T(8,128)(2,1)}, u32[]{:S(2)}) copy-start(bf16[128,4096]{1,0:T(8,128)(2,1)} %copy-done.4) | copy-start | bytes 3145732
  374.9 9.6 %copy-start.16 = (f32[4096]{0:T(1024)S(1)}, f32[4096]{0:T(1024)}, u32[]{:S(2)}) copy-start(f32[4096]{0:T(1024)} %param.6) | copy-start | bytes 49156
  381.9 1.3 copy-start.11
  383.2 1.3 copy-start.13
  384.5 1.2 copy-start.7
  385.7 1.2 copy-start.9
  387.0 1.6 copy-start.12
  388.6 1.6 copy-start.14
  396.5 0.6 copy-start.17

commit v3 on v0

v3 whole, which is shorter than its diff:
```python
import functools

import jax
import jax.numpy as jnp
from jax import lax
from jax.experimental import pallas as pl
from jax.experimental.pallas import tpu as pltpu
from jax.sharding import PartitionSpec as P

STOPS = 4
TEMP = 0.05
EPS = 1e-06
SLOTS = 8
LINE = 8
STRIDE, UNSTRIDE = 27, 19
HOP_STEP = 20
MIB = 1 << 20
MESH = pl.DeviceIdType.MESH
NT = (((1,), (1,)), ((), ()))
TN = (((0,), (0,)), ((), ()))


def dot(a, b, dims=(((1,), (0,)), ((), ()))):
    return lax.dot_general(a, b, dims, preferred_element_type=jnp.float32)


def kernel(
    n, reps, q_ref, p_ref, gain_ref, idx_ref, q_out, p_out, loss_ref, gain_out,
    p_win, q_win, x_send, w, y_send, y_recv, table, sums, q_part, idx_all, asks, asks_t, t_send, t_recv,
    shared, side_send, side_recv, q_norm, p_norm, q_weight, p_weight, gain_slots,
    x_sem, x_sems, idx_sem, idx_got, t_sem, t_got, sh_sem, sh_got, y_sem, y_got,
    chain_sem, chain_got, side_sem, side_got, g_sems, g_got,
):
    me, rep = lax.axis_index("batch"), lax.axis_index("rep")
    rows, width = q_ref.shape
    neg = 3
    places = n * SLOTS

    def ahead(i):
        return lax.rem(me + STRIDE * i, n)

    def behind(i):
        return lax.rem(me + n * STRIDE - STRIDE * i, n)

    def position(device):
        return lax.rem((me + n - device) * UNSTRIDE, n)

    def remote(src, dst, send, recv, device):
        return pltpu.make_async_remote_copy(
            src_ref=src, dst_ref=dst, send_sem=send, recv_sem=recv, device_id=(device, rep), device_id_type=MESH
        )

    barrier = pltpu.get_barrier_semaphore()

    def greet(i, carry):
        pl.semaphore_signal(barrier, inc=1, device_id=(ahead(i), rep), device_id_type=MESH)
        return carry

    lax.fori_loop(1, n, greet, 0)
    for off in range(1, reps):
        pl.semaphore_signal(barrier, inc=1, device_id=(me, lax.rem(rep + off, reps)), device_id_type=MESH)

    def normalize(chunk, carry):
        cut = pl.ds(pl.multiple_of(chunk * 16, 16), 16)
        units = []
        for src, win, norm in ((q_ref, q_win, q_norm), (p_ref, p_win, p_norm)):
            scaled = src[cut, :].astype(jnp.float32) * gain_ref[...]
            length = jnp.sqrt(jnp.sum(scaled * scaled, axis=-1, keepdims=True) + EPS)
            unit = scaled * (1.0 / length)
            win[0, cut, :] = unit.astype(jnp.bfloat16)
            norm[cut, :] = jnp.broadcast_to(1.0 / length, (16, 128))
            units.append(unit)
        low = lax.broadcasted_iota(jnp.int32, (16, 128), 1) < 64
        for tile in range(width // 128):
            q_tile = units[0][:, tile * 128 : (tile + 1) * 128]
            p_tile = units[1][:, tile * 128 : (tile + 1) * 128]
            x_send[2 * tile, cut, :] = jnp.where(low, q_tile, pltpu.roll(p_tile, 64, 1)).astype(jnp.bfloat16)
            x_send[2 * tile + 1, cut, :] = jnp.where(low, pltpu.roll(q_tile, 64, 1), p_tile).astype(jnp.bfloat16)
        return carry

    lax.fori_loop(0, rows // 16, normalize, 0)
    idx_all[0] = idx_ref[...]
    w[0] = x_send[me]
    pl.semaphore_wait(barrier, n - 1 + reps - 1)

    def idx_copy(i):
        return remote(idx_all.at[0], idx_all.at[i], idx_sem, idx_got, ahead(i))

    def x_copy(i):
        return remote(x_send.at[ahead(i)], w.at[i], x_sem, x_sems.at[i], ahead(i))

    def start_idx(i, carry):
        idx_copy(i).start()
        return carry

    def start_x(i, carry):
        x_copy(i).start()
        return carry

    right, left = lax.rem(me + 1, n), lax.rem(me + n - 1, n)

    def hop(turn):
        return (
            remote(p_win.at[turn - 1], p_win.at[turn], chain_sem.at[0, turn - 1], chain_got.at[0, turn - 1], right),
            remote(q_win.at[turn - 1], q_win.at[turn], chain_sem.at[1, turn - 1], chain_got.at[1, turn - 1], left),
        )

    def pass_on(turn):
        for copy in hop(turn):
            copy.wait_recv()
        if turn + 1 < STOPS:
            for copy in hop(turn + 1):
                copy.start()

    lax.fori_loop(1, n, start_idx, 0)
    for copy in hop(1):
        copy.start()
    lax.fori_loop(1, n, start_x, 0)

    others = pl.ds(1, n - 1)

    def all_others(buffer, send, recv):
        return remote(buffer.at[others], buffer.at[others], send, recv, right)

    all_others(idx_all, idx_sem, idx_got).wait_recv()
    wide = idx_all[:, :SLOTS, :].reshape(places, 128).astype(jnp.float32)
    asks[...] = wide.astype(jnp.bfloat16)
    asks_t[...] = wide.T

    def pick(step, carry):
        @pl.when(step == HOP_STEP * n // 64)
        def _():
            pass_on(1)

        picked = []
        for part in range(2):
            pos = 2 * step + part

            @pl.when(pos > 0)
            def _():
                x_copy(pos).wait_recv()

            owner = behind(pos)
            column = (lax.broadcasted_iota(jnp.int32, (128, 128), 0) == owner).astype(jnp.bfloat16)
            asked = dot(asks[...], column)
            lane = lax.broadcasted_iota(jnp.int32, asked.shape, 1).astype(jnp.float32)
            hot = jnp.where(asked == lane, 1.0, 0.0).astype(jnp.bfloat16)
            picked.append(dot(hot, w[pos]).reshape(n, SLOTS, 128))
        both = jnp.concatenate(picked, axis=1).astype(jnp.bfloat16)
        table[:, pl.ds(pl.multiple_of(step * 16, 16), 16), :] = both
        return carry

    lax.fori_loop(0, n // 2, pick, 0)

    def places_of(pos):
        slot = idx_all[pos, SLOTS : 2 * SLOTS, :]
        turned = ((me + n - (slot >> 3)) * UNSTRIDE) & (n - 1)
        return turned * SLOTS + (slot & (SLOTS - 1))

    def t_copy(pos):
        return remote(t_send.at[pos], t_recv.at[n - pos], t_sem, t_got, behind(pos))

    def partial_scores(pos):
        mine = w[pos].astype(jnp.float32)
        lane = lax.broadcasted_iota(jnp.int32, mine.shape, 1)
        query = jnp.where(lane < 64, 0.0, pltpu.roll(mine, 64, 1)).astype(jnp.bfloat16)
        scores = dot(table[pos], query, NT)
        place = lax.broadcasted_iota(jnp.int32, scores.shape, 0)
        slot = places_of(pos)
        parts = [
            jnp.sum(jnp.where(place == slot[k : k + 1], scores, 0.0), axis=0, keepdims=True) for k in range(neg)
        ]
        return jnp.concatenate(parts + [jnp.zeros((8 - neg, rows), jnp.float32)], axis=0)

    def score_step(pos, carry):
        t_send[pos] = partial_scores(pos)
        t_copy(pos).start()
        return carry

    lax.fori_loop(1, n, score_step, 0)
    t_recv[0] = partial_scores(0)

    def window_scores(p_slot, q_slot):
        step = 512

        def add(tile, total):
            cut = pl.ds(pl.multiple_of(tile * step, step), step)
            return total + dot(p_win[p_slot, :, cut], q_win[q_slot, :, cut], NT)

        return lax.fori_loop(0, width // step, add, jnp.zeros((rows, rows), jnp.float32)) / TEMP

    own = window_scores(0, 0)
    eye = lax.broadcasted_iota(jnp.int32, (rows, rows), 0) == lax.broadcasted_iota(jnp.int32, (rows, rows), 1)
    positive = jnp.sum(jnp.where(eye, own, 0.0), axis=0, keepdims=True)
    exps = [jnp.exp(own), jnp.exp(window_scores(1, 0))]
    pass_on(2)
    far = jnp.sum(jnp.exp(window_scores(2, 1)), axis=0, keepdims=True)
    side_send[...] = jnp.broadcast_to(far, side_send.shape)
    side = remote(side_send, side_recv, side_sem, side_got, right)
    side.start()
    exps.append(jnp.exp(window_scores(2, 0)))
    near = sum(jnp.sum(e, axis=0, keepdims=True) for e in exps)

    all_others(t_recv, t_sem, t_got).wait_recv()
    t = lax.fori_loop(0, n, lambda i, total: total + t_recv[i], jnp.zeros((8, rows), jnp.float32)) / TEMP
    exp_t = jnp.exp(t)
    side.wait_recv()
    partition = near + side_recv[:1] + sum(exp_t[k : k + 1] for k in range(neg))
    inverse = 1.0 / partition
    loss_ref[...] = jnp.log(partition) - positive
    v = (exp_t * inverse).astype(jnp.bfloat16).astype(jnp.float32)
    line = lax.broadcasted_iota(jnp.int32, v.shape, 0)
    shared[0] = jnp.where(line < neg, v, jnp.broadcast_to(inverse, v.shape))

    def sh_copy(i):
        return remote(shared.at[0], shared.at[i], sh_sem, sh_got, ahead(i))

    def start_sh(i, carry):
        sh_copy(i).start()
        return carry

    lax.fori_loop(1, n, start_sh, 0)
    for stop in range(STOPS - 1):
        weight = exps[stop] * inverse
        if stop == 0:
            weight = weight - jnp.where(eye, 1.0, 0.0)
            p_weight[0] = weight.astype(jnp.bfloat16)
        q_weight[stop] = weight.T.astype(jnp.bfloat16)
    all_others(shared, sh_sem, sh_got).wait_recv()

    def spread(step, carry):
        grads = []
        for part in range(2):
            pos = 2 * step + part
            place = lax.broadcasted_iota(jnp.int32, (places, rows), 0)
            slot = places_of(pos)
            weight = jnp.zeros((places, rows), jnp.float32)
            for k in range(neg):
                weight = weight + jnp.where(place == slot[k : k + 1], shared[pos, k : k + 1, :], 0.0)
            weight = weight.astype(jnp.bfloat16)
            q_part[pos] = dot(weight, table[pos], TN)
            grads.append((dot(weight, w[pos]) / TEMP).reshape(n, SLOTS, 128))
        both = jnp.concatenate(grads, axis=1).astype(jnp.bfloat16)
        sums[:, pl.ds(pl.multiple_of(step * 16, 16), 16), :] = both
        return carry

    lax.fori_loop(0, n // 2, spread, 0)

    def y_copy(pos):
        return remote(y_send.at[pos], y_recv.at[n - pos], y_sem, y_got, behind(pos))

    def gather_tile(pos):
        asked = asks_t[pl.ds(behind(pos), 1), :]
        target = lax.broadcasted_iota(jnp.int32, (rows, places), 0).astype(jnp.float32)
        hot = jnp.where(target == asked, 1.0, 0.0).astype(jnp.bfloat16)
        p_grad = dot(hot, sums[pos])
        lane = lax.broadcasted_iota(jnp.int32, p_grad.shape, 1)
        return jnp.where(lane < 64, p_grad, q_part[pos] / TEMP).astype(jnp.bfloat16)

    def gather_step(pos, carry):
        y_send[pos] = gather_tile(pos)
        y_copy(pos).start()
        return carry

    lax.fori_loop(1, n, gather_step, 0)
    y_recv[0] = gather_tile(0)

    pass_on(3)

    def inverse_of(stop):
        return shared[position(lax.rem(me + stop, n)), neg : neg + 1, :]

    for stop in range(1, STOPS):
        p_weight[stop] = (jnp.exp(window_scores(0, stop)) * inverse_of(stop)).astype(jnp.bfloat16)
    q_weight[STOPS - 1] = (jnp.exp(window_scores(STOPS - 1, 0)) * inverse).T.astype(jnp.bfloat16)

    def products(tile, carry):
        cut = pl.ds(pl.multiple_of(tile * 256, 256), 256)
        q_grad = jnp.zeros((rows, 256), jnp.float32)
        p_grad = jnp.zeros((rows, 256), jnp.float32)
        for stop in range(STOPS):
            q_grad = q_grad + dot(q_weight[stop], p_win[stop, :, cut])
            p_grad = p_grad + dot(p_weight[stop], q_win[stop, :, cut])
        q_out[:, cut] = q_grad / TEMP
        p_out[:, cut] = p_grad / TEMP
        return carry

    lax.fori_loop(0, width // 256, products, 0)

    all_others(y_recv, y_sem, y_got).wait_recv()

    def finish(chunk, total):
        cut = pl.ds(pl.multiple_of(chunk * 16, 16), 16)
        low = lax.broadcasted_iota(jnp.int32, (16, 128), 1) < 64
        q_tiles, p_tiles = [], []
        for tile in range(width // 128):
            even = y_recv[position(2 * tile), cut, :].astype(jnp.float32)
            odd = y_recv[position(2 * tile + 1), cut, :].astype(jnp.float32)
            p_tiles.append(jnp.where(low, even, pltpu.roll(odd, 64, 1)))
            q_tiles.append(jnp.where(low, pltpu.roll(even, 64, 1), odd))
        for src, norm, tiles, out in ((q_ref, q_norm, q_tiles, q_out), (p_ref, p_norm, p_tiles, p_out)):
            hidden = src[cut, :].astype(jnp.float32)
            over = norm[cut, :1]
            gain = gain_ref[...]
            unit = hidden * gain * over
            grad = out[cut, :] + jnp.concatenate(tiles, axis=1)
            inner = jnp.sum(unit * grad, axis=-1, keepdims=True)
            scaled = (grad - unit * inner) * over
            out[cut, :] = scaled * gain
            total = total + jnp.sum(hidden * scaled, axis=0, keepdims=True)
        return total

    gain_part = lax.fori_loop(0, rows // 16, finish, jnp.zeros((1, width), jnp.float32))

    for tile in range(width // 128):
        gain_out[tile : tile + 1, :] = gain_part[:, tile * 128 : (tile + 1) * 128]
    z, row = lax.rem(me, LINE), me // LINE
    plan = (
        (z, LINE, lambda i: (row * LINE + i, rep)),
        (row, n // LINE, lambda i: (i * LINE + z, rep)),
        (rep, reps, lambda i: (me, i)),
    )
    for turn, (here, size, target) in enumerate(plan):
        gain_slots[turn, here] = gain_out[...]

        def g_copy(off, slot):
            return pltpu.make_async_remote_copy(
                src_ref=gain_slots.at[turn, slot],
                dst_ref=gain_slots.at[turn, slot],
                send_sem=g_sems.at[turn, off],
                recv_sem=g_got.at[turn, slot],
                device_id=target(lax.rem(here + off, size)),
                device_id_type=MESH,
            )

        for off in range(1, size):
            g_copy(off, here).start()
        for off in range(1, size):
            g_copy(off, lax.rem(here + off, size)).wait_recv()
        total = gain_slots[turn, 0]
        for i in range(1, size):
            total = total + gain_slots[turn, i]
        gain_out[...] = total
        for off in range(1, size):
            g_copy(off, here).wait_send()

    all_others(idx_all, idx_sem, idx_got).wait_send()
    all_others(x_send, x_sem, idx_got).wait_send()
    all_others(t_send, t_sem, t_got).wait_send()
    all_others(shared, sh_sem, sh_got).wait_send()
    all_others(y_send, y_sem, y_got).wait_send()
    side.wait_send()
    for turn in range(1, STOPS):
        for copy in hop(turn):
            copy.wait_send()


def run(q_hidden, p_hidden, gain, idx):
    n, reps = lax.axis_size("batch"), lax.axis_size("rep")
    rows, width = q_hidden.shape
    places = n * SLOTS
    vmem = pl.BlockSpec(memory_space=pltpu.VMEM)
    bf16, f32 = jnp.bfloat16, jnp.float32
    dma = pltpu.SemaphoreType.DMA
    most = max(LINE, n // LINE, reps)
    return pl.pallas_call(
        functools.partial(kernel, n, reps),
        in_specs=[vmem] * 4,
        out_specs=[vmem] * 4,
        out_shape=[
            jax.ShapeDtypeStruct((rows, width), f32),
            jax.ShapeDtypeStruct((rows, width), f32),
            jax.ShapeDtypeStruct((1, rows), f32),
            jax.ShapeDtypeStruct((width // 128, 128), f32),
        ],
        scratch_shapes=[
            pltpu.VMEM((STOPS, rows, width), bf16),
            pltpu.VMEM((STOPS, rows, width), bf16),
            pltpu.VMEM((n, rows, 128), bf16),
            pltpu.VMEM((n, rows, 128), bf16),
            pltpu.VMEM((n, rows, 128), bf16),
            pltpu.VMEM((n, rows, 128), bf16),
            pltpu.VMEM((n, places, 128), bf16),
            pltpu.VMEM((n, places, 128), bf16),
            pltpu.VMEM((n, rows, 128), f32),
            pltpu.VMEM((n, 2 * SLOTS, 128), jnp.int32),
            pltpu.VMEM((places, 128), bf16),
            pltpu.VMEM((128, places), f32),
            pltpu.VMEM((n, 8, rows), f32),
            pltpu.VMEM((n, 8, rows), f32),
            pltpu.VMEM((n, 8, rows), f32),
            pltpu.VMEM((8, rows), f32),
            pltpu.VMEM((8, rows), f32),
            pltpu.VMEM((rows, 128), f32),
            pltpu.VMEM((rows, 128), f32),
            pltpu.VMEM((STOPS, rows, rows), bf16),
            pltpu.VMEM((STOPS, rows, rows), bf16),
            pltpu.VMEM((3, most, width // 128, 128), f32),
            dma,
            dma((n,)),
            dma,
            dma,
            dma,
            dma,
            dma,
            dma,
            dma,
            dma,
            dma((2, STOPS - 1)),
            dma((2, STOPS - 1)),
            dma,
            dma,
            dma((3, most)),
            dma((3, most)),
        ],
        compiler_params=pltpu.CompilerParams(
            collective_id=0, has_side_effects=True, vmem_limit_bytes=60 * MIB
        ),
        name="contrastive",
    )(q_hidden, p_hidden, gain.reshape(1, width), idx)


def slot_tables(wanted, peers):
    rows, neg = wanted.shape
    flat = wanted.T.reshape(-1)
    count = flat.shape[0]
    owner = flat // rows
    place = jnp.arange(count, dtype=jnp.int32)
    same = flat[:, None] == flat[None, :]
    again = jnp.any(same & (place[None, :] < place[:, None]), axis=1)
    smaller = (owner[:, None] == owner[None, :]) & (flat[:, None] < flat[None, :])
    rank = jnp.sum((smaller & ~again[:, None]).astype(jnp.int32), axis=0)
    slot = owner * SLOTS + rank
    key = rank * 128 + owner
    cells = jnp.arange(SLOTS * 128, dtype=jnp.int32)
    hit = (key[None, :] == cells[:, None]) & ~again[None, :]
    named = jnp.sum(jnp.where(hit, flat[None, :] % rows + 1, 0), axis=1) - 1
    pad = jnp.full((SLOTS - neg, rows), -1, jnp.int32)
    return jnp.concatenate([named.reshape(SLOTS, 128), slot.reshape(neg, rows), pad], axis=0)


def local(query_hidden, passage_hidden, norm_gain, negatives):
    idx = slot_tables(negatives[0], lax.axis_size("batch"))
    query_grad, passage_grad, loss, gain_grad = run(query_hidden[0], passage_hidden[0], norm_gain, idx)
    return (query_grad[None], passage_grad[None], loss, gain_grad.reshape(norm_gain.shape))


def solution(mesh):
    return jax.shard_map(
        local,
        mesh=mesh,
        in_specs=(P("rep", "batch", None), P("rep", "batch", None), P(), P("rep", "batch", None)),
        out_specs=(P("rep", "batch", None), P("rep", "batch", None), P("rep", "batch"), P()),
        check_vma=False,
    )
```

time: 948 us -> 248 us (0.26); the launches traced: 938 us -> 248 us
  waiting for transfers between devices: 531 us -> 0 us
  Pallas kernels: 0 us -> 238 us
  local copies, waits for them, and re-layouts: 223 us -> 6.47 us
  blocking collectives: 78.6 us -> 0 us
  matrix products: 47.8 us -> 0 us
  starting transfers between devices: 37.9 us -> 0 us
  other arithmetic: 18.8 us -> 2.94 us
    ppermute x6 -> x0, waiting for transfers between devices: 372 us -> none  [from_behind(): return lax.ppermute(block, axis, route)]
    pallas_call x0 -> x1, Pallas kernels: none -> 238 us  [run(): pl.pallas_call(functools.partial(kernel, n, reps), in_specs=[vmem] * 4, o...]
    all_to_all x3 -> x0, waiting for transfers between devices: 159 us -> none  [the longest x1 152 us: local(): lax.all_to_all(outgoing, 'batch', split_axis=0, concat_axis=0, tiled=True)]
    scatter x3 -> x0, local copies, waits for them, and re-layouts: 132 us -> none  [the longest x2 112 us: local(): outgoing = jnp.zeros((peer_count, capacity, feat_width), jnp.bfloat16).at...]
    psum x1 -> x0, blocking collectives: 78.6 us -> none  [local(): gain_grad = lax.psum(gain_query + gain_passage, ('batch', 'rep'))]
    dot_general x7 -> x0, matrix products: 47.8 us -> none  [the longest x1 14.1 us: local(): jnp.dot(same_index.astype(jnp.float32), neg_rows, precision=lax.Precision...]
    gather x4 -> x0, local copies, waits for them, and re-layouts: 34.9 us -> none  [the longest x1 17.7 us: local(): fetched = arrived[owner_dev, slot_each]]
    all_to_all x3 -> x0, starting transfers between devices: 26.6 us -> none  [the longest x1 15.1 us: local(): lax.all_to_all(request, 'batch', split_axis=0, concat_axis=0, tiled=True)]
  transfers between devices with their start and end apart: 9 -> 0, of which waited for: 8 -> 0; matrix products, arithmetic and copies ran while one was open for 6% -> 0% of each run, Pallas kernels for 0% -> 0%
where the time goes in v3:
time: 248 us
  Pallas kernels  238 us (96%)
  local copies, waits for them, and re-layouts  6.47 us (3%)
  other arithmetic  2.94 us (1%)
    pallas_call x1, Pallas kernels, run(): pl.pallas_call(functools.partial(kernel, n, reps), in_specs=[vmem] * 4, o...  238 us
    unnamed x11, local copies, waits for them, and re-layouts  6.39 us

profile of v3, /device:TPU:1, one launch (start us, length us, event | category | flops | bytes accessed | tf_op | source)
XLA Modules:
  0.0 247.8 jit_solution(6097470439933311908)
XLA Ops:
  0.6 0.1 pad.2.clone
  0.7 0.7 copy.33
  1.4 0.2 fusion.2
  1.6 0.7 fusion.6
  2.3 0.2 convert_reduce_fusion
  2.6 0.4 select_reduce_fusion
  3.0 0.7 fusion.9
  3.7 0.7 add_add_fusion.idx_ref
  4.4 237.7 %contrastive.1 = (f32[128,4096]{1,0:T(8,128)}, f32[128,4096]{1,0:T(8,128)}, f32[1,128]{1,0:T(1,128)}, f32[32,128]{1,0:T(8,128)}) custom-call(bf16[128,4096]{1,0:T(8,128)(2,1)} %bitcast.43, bf16[128,4096]{1,0:T(8,128)(2,1)} %bitcast.44, f32[1,4096]{1,0:T(1,128)} %bitcast.47, s32[16,128]{1,0:T(8,128)} %add_add_fusion.idx_ref), custom_call_target="tpu_custom_call" | custom-call | tf_op jit(solution)/shard_map/contrastive/pallas_call | solution.py:366
  242.1 0.0 copy-start
  242.1 3.3 %copy.38 = f32[1,128,4096]{2,1,0:T(8,128)} copy(f32[1,128,4096]{2,1,0:T(8,128)} %bitcast.42) | data formatting | bytes 4194304
  245.3 0.0 copy-done
  245.3 0.0 copy-start.2
  245.3 0.0 copy-start.1
  245.4 1.3 copy.39
  246.7 0.0 copy-done.2
  246.7 0.5 copy.40
  247.2 0.0 copy-done.1
  247.2 0.6 copy.41
  (4 shorter events, 0.0 us)
Async XLA Ops:
  242.1 3.3 %copy-start = (f32[128,4096]{1,0:T(8,128)S(1)}, f32[128,4096]{1,0:T(8,128)}, u32[]{:S(2)}) copy-start(f32[128,4096]{1,0:T(8,128)} %get-tuple-element.9) | copy-start | bytes 6291460
  245.3 1.3 copy-start.2
  245.3 1.8 copy-start.1

commit v4 on v3

v4 whole, which is shorter than its diff:
```python
import functools

import jax
import jax.numpy as jnp
from jax import lax
from jax.experimental import pallas as pl
from jax.experimental.pallas import tpu as pltpu
from jax.sharding import PartitionSpec as P

STOPS = 4
TEMP = 0.05
EPS = 1e-06
SLOTS = 8
LINE = 8
STRIDE, UNSTRIDE = 27, 19
FIRST_HOP = (22, 27)
SECOND_HOP = (20, 50)
MIB = 1 << 20
MESH = pl.DeviceIdType.MESH
NT = (((1,), (1,)), ((), ()))
TN = (((0,), (0,)), ((), ()))


def dot(a, b, dims=(((1,), (0,)), ((), ()))):
    return lax.dot_general(a, b, dims, preferred_element_type=jnp.float32)


def kernel(
    n, reps, q_hbm, p_hbm, gain_ref, idx_ref, q_out, p_out, loss_ref, gain_out,
    q_ref, p_ref, q_acc, p_acc, p_win, q_win, x_send, w, yq_send, yq_recv, yp_send, yp_recv, table, sums,
    idx_all, asks, asks_t, t_send, t_recv, shared, side_send, side_recv, q_norm, p_norm, q_weight, p_weight,
    gain_part, gain_near, gain_far, gain_all,
    in_sems, out_sems, x_sem, x_sems, idx_sem, idx_got, t_sem, t_got, sh_sem, sh_sems, yq_sem, yq_got, yp_sem, yp_got,
    chain_sem, chain_got, side_sem, side_got, g_sems, g_got,
):
    me, rep = lax.axis_index("batch"), lax.axis_index("rep")
    rows, width = q_ref.shape
    half = rows // 2
    neg = 3
    places = n * SLOTS
    tiles = width // 128

    def ahead(i):
        return lax.rem(me + STRIDE * i, n)

    def behind(i):
        return lax.rem(me + n * STRIDE - STRIDE * i, n)

    def position(device):
        return lax.rem((me + n - device) * UNSTRIDE, n)

    def remote(src, dst, send, recv, device, group=rep):
        return pltpu.make_async_remote_copy(
            src_ref=src, dst_ref=dst, send_sem=send, recv_sem=recv, device_id=(device, group), device_id_type=MESH
        )

    inputs = (pltpu.make_async_copy(q_hbm, q_ref, in_sems.at[0]), pltpu.make_async_copy(p_hbm, p_ref, in_sems.at[1]))
    for copy in inputs:
        copy.start()

    barrier = pltpu.get_barrier_semaphore()
    z, row = lax.rem(me, LINE), me // LINE
    lines = n // LINE

    def greet(i, carry):
        pl.semaphore_signal(barrier, inc=1, device_id=(ahead(i), rep), device_id_type=MESH)
        return carry

    def greet_group(i, carry):
        group = lax.rem(rep + 1 + i // lines, reps)
        device = lax.rem(i, lines) * LINE + z
        pl.semaphore_signal(barrier, inc=1, device_id=(device, group), device_id_type=MESH)
        return carry

    lax.fori_loop(1, n, greet, 0)
    lax.fori_loop(0, (reps - 1) * lines, greet_group, 0)
    for copy in inputs:
        copy.wait()

    def normalize(chunk, carry):
        cut = pl.ds(pl.multiple_of(chunk * 16, 16), 16)
        units = []
        for src, win, norm in ((q_ref, q_win, q_norm), (p_ref, p_win, p_norm)):
            scaled = src[cut, :].astype(jnp.float32) * gain_ref[...]
            length = jnp.sqrt(jnp.sum(scaled * scaled, axis=-1, keepdims=True) + EPS)
            unit = scaled * (1.0 / length)
            win[0, cut, :] = unit.astype(jnp.bfloat16)
            norm[cut, :] = jnp.broadcast_to(1.0 / length, (16, 128))
            units.append(unit)
        low = lax.broadcasted_iota(jnp.int32, (16, 128), 1) < 64
        for tile in range(tiles):
            q_tile = units[0][:, tile * 128 : (tile + 1) * 128]
            p_tile = units[1][:, tile * 128 : (tile + 1) * 128]
            x_send[2 * tile, cut, :] = jnp.where(low, q_tile, pltpu.roll(p_tile, 64, 1)).astype(jnp.bfloat16)
            x_send[2 * tile + 1, cut, :] = jnp.where(low, pltpu.roll(q_tile, 64, 1), p_tile).astype(jnp.bfloat16)
        return carry

    lax.fori_loop(0, rows // 16, normalize, 0)
    w[0] = x_send[me]
    pl.semaphore_wait(barrier, n - 1 + (reps - 1) * lines)

    def x_copy(i):
        return remote(x_send.at[ahead(i)], w.at[i], x_sem, x_sems.at[i], ahead(i))

    def start_x(i, carry):
        x_copy(i).start()
        return carry

    lax.fori_loop(1, n, start_x, 0)

    flat = idx_ref[...]
    flat_f = flat.astype(jnp.float32)
    owner_row = (flat >> 7).astype(jnp.float32)
    columns = jnp.concatenate([flat_f, jnp.zeros((rows - neg, rows), jnp.float32)], axis=0).T
    owner_columns = (columns.astype(jnp.int32) >> 7).astype(jnp.float32)
    down = lax.broadcasted_iota(jnp.int32, (rows, rows), 0)
    across = lax.broadcasted_iota(jnp.int32, (rows, rows), 1)
    again_row, again_column, ranks = [], [], []
    for k in range(neg):
        seen = jnp.zeros((rows, rows), jnp.float32)
        seen_t = jnp.zeros((rows, rows), jnp.float32)
        for j in range(k + 1):
            same = columns[:, j : j + 1] == flat_f[k : k + 1]
            same_t = columns[:, k : k + 1] == flat_f[j : j + 1]
            if j == k:
                same, same_t = same & (down < across), same_t & (across < down)
            seen = seen + jnp.where(same, 1.0, 0.0)
            seen_t = seen_t + jnp.where(same_t, 1.0, 0.0)
        again_row.append(jnp.sum(seen, axis=0, keepdims=True))
        again_column.append(jnp.sum(seen_t, axis=1, keepdims=True))
    for k in range(neg):
        count = jnp.zeros((rows, rows), jnp.float32)
        for j in range(neg):
            lower = (owner_columns[:, j : j + 1] == owner_row[k : k + 1]) & (columns[:, j : j + 1] < flat_f[k : k + 1])
            count = count + jnp.where(lower & (again_column[j] == 0.0), 1.0, 0.0)
        ranks.append(jnp.sum(count, axis=0, keepdims=True))
    named = jnp.zeros((SLOTS, 128), jnp.float32)
    at_rank = lax.broadcasted_iota(jnp.int32, (SLOTS, rows), 0).astype(jnp.float32)
    for k in range(neg):
        first = (at_rank == ranks[k]) & (again_row[k] == 0.0)
        value = jnp.where(first, (flat[k : k + 1] & 127).astype(jnp.float32) + 1.0, 0.0).astype(jnp.bfloat16)
        at_owner = jnp.where(owner_columns[:, k : k + 1] == across.astype(jnp.float32), 1.0, 0.0).astype(jnp.bfloat16)
        named = named + dot(value, at_owner)
    lines_of = [named - 1.0, owner_row] + ranks + [jnp.zeros((2, 128), jnp.float32)]
    idx_all[0] = jnp.concatenate(lines_of, axis=0).astype(jnp.bfloat16)
    own_entry = flat == me * rows + lax.broadcasted_iota(jnp.int32, flat.shape, 1)

    def start_idx(i, carry):
        remote(idx_all.at[0], idx_all.at[i], idx_sem, idx_got, ahead(i)).start()
        return carry

    lax.fori_loop(1, n, start_idx, 0)

    right, left = lax.rem(me + 1, n), lax.rem(me + n - 1, n)

    def hop(turn, part):
        cut = pl.ds(part * half, half)
        sems = [(chain_sem.at[way, turn - 1, part], chain_got.at[way, turn - 1, part]) for way in range(2)]
        return (
            remote(p_win.at[turn - 1, cut], p_win.at[turn, cut], *sems[0], right),
            remote(q_win.at[turn - 1, cut], q_win.at[turn, cut], *sems[1], left),
        )

    def start_hop(turn, part):
        for copy in hop(turn, part):
            copy.start()

    def pass_on(turn, part):
        for copy in hop(turn, part):
            copy.wait_recv()
        if turn + 1 < STOPS:
            start_hop(turn + 1, part)

    others = pl.ds(1, n - 1)

    def all_others(buffer, send, recv):
        return remote(buffer.at[others], buffer.at[others], send, recv, right)

    all_others(idx_all, idx_sem, idx_got).wait_recv()
    wide = idx_all[...].astype(jnp.float32)[:, :SLOTS, :].reshape(places, 128)
    asks[...] = wide.astype(jnp.bfloat16)
    asks_t[...] = wide.T

    def pick(step, carry):
        for part in range(2):

            @pl.when(step == FIRST_HOP[part] * n // 64)
            def _():
                start_hop(1, part)

        picked = []
        for part in range(2):
            pos = 2 * step + part

            @pl.when(pos > 0)
            def _():
                x_copy(pos).wait_recv()

            owner = behind(pos)
            column = (lax.broadcasted_iota(jnp.int32, (128, 128), 0) == owner).astype(jnp.bfloat16)
            asked = dot(asks[...], column)
            lane = lax.broadcasted_iota(jnp.int32, asked.shape, 1).astype(jnp.float32)
            hot = jnp.where(asked == lane, 1.0, 0.0).astype(jnp.bfloat16)
            picked.append(dot(hot, w[pos]).reshape(n, SLOTS, 128))
        both = jnp.concatenate(picked, axis=1).astype(jnp.bfloat16)
        table[:, pl.ds(pl.multiple_of(step * 16, 16), 16), :] = both
        return carry

    lax.fori_loop(0, n // 2, pick, 0)

    def places_of(pos):
        entry = idx_all[pos].astype(jnp.float32).astype(jnp.int32)
        owner, rank = entry[SLOTS : SLOTS + neg], entry[SLOTS + neg : SLOTS + 2 * neg]
        return (((me + n - owner) * UNSTRIDE) & (n - 1)) * SLOTS + rank

    def t_copy(pos):
        return remote(t_send.at[pos], t_recv.at[n - pos], t_sem, t_got, behind(pos))

    def partial_scores(pos):
        mine = w[pos].astype(jnp.float32)
        lane = lax.broadcasted_iota(jnp.int32, mine.shape, 1)
        query = jnp.where(lane < 64, 0.0, pltpu.roll(mine, 64, 1)).astype(jnp.bfloat16)
        scores = dot(table[pos], query, NT)
        place = lax.broadcasted_iota(jnp.int32, scores.shape, 0)
        slot = places_of(pos)
        parts = [
            jnp.sum(jnp.where(place == slot[k : k + 1], scores, 0.0), axis=0, keepdims=True) for k in range(neg)
        ]
        return jnp.concatenate(parts + [jnp.zeros((8 - neg, rows), jnp.float32)], axis=0)

    def score_step(pos, carry):
        for part in range(2):

            @pl.when(pos == SECOND_HOP[part] * n // 64)
            def _():
                pass_on(1, part)

        t_send[pos] = partial_scores(pos)
        t_copy(pos).start()
        return carry

    lax.fori_loop(1, n, score_step, 0)
    t_recv[0] = partial_scores(0)

    def window_scores(p_slot, q_slot, p_rows=(0, rows), q_count=1):
        step = 512

        def add(tile, total):
            cut = pl.ds(pl.multiple_of(tile * step, step), step)
            down_block = p_win[p_slot, p_rows[0] : p_rows[0] + p_rows[1], cut]
            across_block = q_win[q_slot : q_slot + q_count, :, cut].reshape(q_count * rows, step)
            return total + dot(down_block, across_block, NT)

        start = jnp.zeros((p_rows[1], q_count * rows), jnp.float32)
        return lax.fori_loop(0, width // step, add, start) / TEMP

    own = window_scores(0, 0)
    eye = down == across
    positive = jnp.sum(jnp.where(eye, own, 0.0), axis=0, keepdims=True)
    exps = [jnp.exp(own), jnp.exp(window_scores(1, 0))]
    pass_on(2, 0)
    upper = jnp.exp(window_scores(2, 0, (0, half), 2))
    pass_on(2, 1)
    lower = jnp.exp(window_scores(2, 0, (half, half), 2))
    far = jnp.sum(upper[:, rows:], axis=0, keepdims=True) + jnp.sum(lower[:, rows:], axis=0, keepdims=True)
    side_send[...] = jnp.broadcast_to(far, side_send.shape)
    side = remote(side_send, side_recv, side_sem, side_got, right)
    side.start()
    exps.append(jnp.concatenate([upper[:, :rows], lower[:, :rows]], axis=0))
    near = sum(jnp.sum(e, axis=0, keepdims=True) for e in exps)

    all_others(t_recv, t_sem, t_got).wait_recv()
    t = lax.fori_loop(0, n, lambda i, total: total + t_recv[i], jnp.zeros((8, rows), jnp.float32)) / TEMP
    exp_t = jnp.exp(t)
    side.wait_recv()
    partition = near + side_recv[:1] + sum(exp_t[k : k + 1] for k in range(neg))
    inverse = 1.0 / partition
    v = (exp_t[:neg] * inverse).astype(jnp.bfloat16).astype(jnp.float32)
    own_v = jnp.sum(jnp.where(own_entry, v, 0.0), axis=0, keepdims=True)
    v = jnp.where(own_entry, -v, v)
    shared[0] = jnp.concatenate([v, jnp.broadcast_to(inverse, (8 - neg, rows))], axis=0)

    def sh_copy(i):
        return remote(shared.at[0], shared.at[i], sh_sem, sh_sems.at[i], ahead(i))

    def start_sh(i, carry):
        sh_copy(i).start()
        return carry

    lax.fori_loop(1, n, start_sh, 0)
    loss_ref[...] = jnp.log(partition) - positive
    for stop in range(STOPS - 1):
        weight = exps[stop] * inverse
        if stop == 0:
            weight = (weight - jnp.where(eye, 1.0, 0.0)).astype(jnp.bfloat16).astype(jnp.float32)
            p_weight[0] = weight.astype(jnp.bfloat16)
            weight = weight + jnp.where(eye, own_v, 0.0)
        q_weight[stop] = weight.T.astype(jnp.bfloat16)

    def yq_copy(pos):
        return remote(yq_send.at[pos], yq_recv.at[n - pos], yq_sem, yq_got, behind(pos))

    def fold(block, lanes):
        first, second = block[:half], block[half:]
        low = lax.broadcasted_iota(jnp.int32, (half, 128), 1) < 64
        if lanes == 0:
            return jnp.where(low, first, pltpu.roll(second, 64, 1)).astype(jnp.bfloat16)
        return jnp.where(low, pltpu.roll(first, 64, 1), second).astype(jnp.bfloat16)

    def spread(step, carry):
        grads = []
        for part in range(2):
            pos = 2 * step + part

            @pl.when(pos > 0)
            def _():
                sh_copy(pos).wait_recv()

            place = lax.broadcasted_iota(jnp.int32, (places, rows), 0)
            slot = places_of(pos)
            weight = jnp.zeros((places, rows), jnp.float32)
            for k in range(neg):
                weight = weight + jnp.where(place == slot[k : k + 1], shared[pos, k : k + 1, :], 0.0)
            q_side = jnp.maximum(weight, 0.0).astype(jnp.bfloat16)
            p_side = jnp.abs(weight).astype(jnp.bfloat16)
            yq_send[pos] = fold(dot(q_side, table[pos], TN) / TEMP, 64)

            @pl.when(pos > 0)
            def _():
                yq_copy(pos).start()

            grads.append((dot(p_side, w[pos]) / TEMP).reshape(n, SLOTS, 128))
        both = jnp.concatenate(grads, axis=1).astype(jnp.bfloat16)
        sums[:, pl.ds(pl.multiple_of(step * 16, 16), 16), :] = both
        return carry

    lax.fori_loop(0, n // 2, spread, 0)
    yq_recv[0] = yq_send[0]

    def yp_copy(pos):
        return remote(yp_send.at[pos], yp_recv.at[n - pos], yp_sem, yp_got, behind(pos))

    def gather_tile(pos):
        asked = asks_t[pl.ds(behind(pos), 1), :]
        target = lax.broadcasted_iota(jnp.int32, (rows, places), 0).astype(jnp.float32)
        hot = jnp.where(target == asked, 1.0, 0.0).astype(jnp.bfloat16)
        return fold(dot(hot, sums[pos]), 0)

    def gather_step(pos, carry):
        yp_send[pos] = gather_tile(pos)
        yp_copy(pos).start()
        return carry

    lax.fori_loop(1, n, gather_step, 0)
    yp_recv[0] = gather_tile(0)

    pass_on(3, 0)
    pass_on(3, 1)

    def inverse_of(stop):
        return shared[position(lax.rem(me + stop, n)), neg : neg + 1, :]

    for stop in range(1, STOPS):
        p_weight[stop] = (jnp.exp(window_scores(0, stop)) * inverse_of(stop)).astype(jnp.bfloat16)
    q_weight[STOPS - 1] = (jnp.exp(window_scores(STOPS - 1, 0)) * inverse).T.astype(jnp.bfloat16)

    def products(tile, carry):
        cut = pl.ds(pl.multiple_of(tile * 256, 256), 256)
        q_grad = jnp.zeros((rows, 256), jnp.float32)
        p_grad = jnp.zeros((rows, 256), jnp.float32)
        for stop in range(STOPS):
            q_grad = q_grad + dot(q_weight[stop], p_win[stop, :, cut])
            p_grad = p_grad + dot(p_weight[stop], q_win[stop, :, cut])
        q_acc[:, cut] = q_grad / TEMP
        p_acc[:, cut] = p_grad / TEMP
        return carry

    lax.fori_loop(0, width // 256, products, 0)

    all_others(yq_recv, yq_sem, yq_got).wait_recv()
    all_others(yp_recv, yp_sem, yp_got).wait_recv()

    def finish(chunk, total):
        cut = pl.ds(pl.multiple_of(chunk * 16, 16), 16)
        upper_cut = pl.ds(pl.multiple_of(half + chunk * 16, 16), 16)
        low = lax.broadcasted_iota(jnp.int32, (16, 128), 1) < 64
        for src, norm, recv, out in ((q_ref, q_norm, yq_recv, q_acc), (p_ref, p_norm, yp_recv, p_acc)):
            for tile in range(tiles):
                lanes = slice(tile * 128, (tile + 1) * 128)
                even = recv[position(2 * tile), cut, :].astype(jnp.float32)
                odd = recv[position(2 * tile + 1), cut, :].astype(jnp.float32)
                out[cut, lanes] += jnp.where(low, even, pltpu.roll(odd, 64, 1))
                out[upper_cut, lanes] += jnp.where(low, pltpu.roll(even, 64, 1), odd)
            for here in (cut, upper_cut):
                hidden = src[here, :].astype(jnp.float32)
                over = norm[here, :1]
                gain = gain_ref[...]
                unit = hidden * gain * over
                grad = out[here, :]
                inner = jnp.sum(unit * grad, axis=-1, keepdims=True)
                scaled = (grad - unit * inner) * over
                out[here, :] = scaled * gain
                each = hidden * scaled
                total = total + each[:8] + each[8:]
        return total

    total = lax.fori_loop(0, half // 16, finish, jnp.zeros((8, width), jnp.float32))

    total = jnp.sum(total, axis=0, keepdims=True)
    each = max(1, tiles // LINE)
    gain_part[...] = jnp.zeros_like(gain_part)
    for tile in range(tiles):
        gain_part[tile // each, tile % each : tile % each + 1, :] = total[:, tile * 128 : (tile + 1) * 128]
    outputs = (pltpu.make_async_copy(q_acc, q_out, out_sems.at[0]), pltpu.make_async_copy(p_acc, p_out, out_sems.at[1]))

    def near_copy(off):
        to = lax.rem(z + off, LINE)
        return remote(gain_part.at[to], gain_near.at[off], g_sems.at[0], g_got.at[0], row * LINE + to)

    size = lines * reps
    spot = row * reps + rep

    def far_copy(off):
        to = lax.rem(spot + off, size)
        return remote(
            gain_far.at[0], gain_far.at[off], g_sems.at[1], g_got.at[1], to // reps * LINE + z, lax.rem(to, reps)
        )

    def all_copy(off):
        to = lax.rem(z + off, LINE)
        return remote(gain_all.at[0], gain_all.at[off], g_sems.at[2], g_got.at[2], row * LINE + to)

    def whole(buffer, turn):
        cut = pl.ds(1, buffer.shape[0] - 1)
        return remote(buffer.at[cut], buffer.at[cut], g_sems.at[turn], g_got.at[turn], right)

    for off in range(1, LINE):
        near_copy(off).start()
    for copy in outputs:
        copy.start()
    whole(gain_near, 0).wait_recv()
    piece = gain_part[z]
    for off in range(1, LINE):
        piece = piece + gain_near[off]
    gain_far[0] = piece

    def start_far(off, carry):
        far_copy(off).start()
        return carry

    lax.fori_loop(1, size, start_far, 0)
    whole(gain_far, 1).wait_recv()
    gain_all[0] = lax.fori_loop(
        0, size, lambda i, add: add + gain_far[lax.rem(spot + size - i, size)], jnp.zeros((8, 128), jnp.float32)
    )
    for off in range(1, LINE):
        all_copy(off).start()
    whole(gain_all, 2).wait_recv()
    for tile in range(tiles):
        gain_out[tile : tile + 1, :] = gain_all[lax.rem(z + LINE - tile // each, LINE), tile % each : tile % each + 1, :]

    all_others(idx_all, idx_sem, idx_got).wait_send()
    all_others(x_send, x_sem, idx_got).wait_send()
    all_others(t_send, t_sem, t_got).wait_send()
    all_others(shared, sh_sem, idx_got).wait_send()
    all_others(yq_send, yq_sem, yq_got).wait_send()
    all_others(yp_send, yp_sem, yp_got).wait_send()
    side.wait_send()
    for turn in range(1, STOPS):
        for part in range(2):
            for copy in hop(turn, part):
                copy.wait_send()
    for turn, buffer in enumerate((gain_near, gain_far, gain_all)):
        whole(buffer, turn).wait_send()
    for copy in outputs:
        copy.wait()


def run(q_hidden, p_hidden, gain, idx):
    n, reps = lax.axis_size("batch"), lax.axis_size("rep")
    rows, width = q_hidden.shape
    half = rows // 2
    places = n * SLOTS
    vmem, hbm = pl.BlockSpec(memory_space=pltpu.VMEM), pl.BlockSpec(memory_space=pl.ANY)
    bf16, f32 = jnp.bfloat16, jnp.float32
    dma = pltpu.SemaphoreType.DMA
    return pl.pallas_call(
        functools.partial(kernel, n, reps),
        in_specs=[hbm, hbm, vmem, vmem],
        out_specs=[hbm, hbm, vmem, vmem],
        out_shape=[
            jax.ShapeDtypeStruct((rows, width), f32),
            jax.ShapeDtypeStruct((rows, width), f32),
            jax.ShapeDtypeStruct((1, rows), f32),
            jax.ShapeDtypeStruct((width // 128, 128), f32),
        ],
        scratch_shapes=[
            pltpu.VMEM((rows, width), bf16),
            pltpu.VMEM((rows, width), bf16),
            pltpu.VMEM((rows, width), f32),
            pltpu.VMEM((rows, width), f32),
            pltpu.VMEM((STOPS, rows, width), bf16),
            pltpu.VMEM((STOPS, rows, width), bf16),
            pltpu.VMEM((n, rows, 128), bf16),
            pltpu.VMEM((n, rows, 128), bf16),
            pltpu.VMEM((n, half, 128), bf16),
            pltpu.VMEM((n, half, 128), bf16),
            pltpu.VMEM((n, half, 128), bf16),
            pltpu.VMEM((n, half, 128), bf16),
            pltpu.VMEM((n, places, 128), bf16),
            pltpu.VMEM((n, places, 128), bf16),
            pltpu.VMEM((n, 2 * SLOTS, 128), bf16),
            pltpu.VMEM((places, 128), bf16),
            pltpu.VMEM((128, places), f32),
            pltpu.VMEM((n, 8, rows), f32),
            pltpu.VMEM((n, 8, rows), f32),
            pltpu.VMEM((n, 8, rows), f32),
            pltpu.VMEM((8, rows), f32),
            pltpu.VMEM((8, rows), f32),
            pltpu.VMEM((rows, 128), f32),
            pltpu.VMEM((rows, 128), f32),
            pltpu.VMEM((STOPS, rows, rows), bf16),
            pltpu.VMEM((STOPS, rows, rows), bf16),
            pltpu.VMEM((LINE, 8, 128), f32),
            pltpu.VMEM((LINE, 8, 128), f32),
            pltpu.VMEM((n // LINE * reps, 8, 128), f32),
            pltpu.VMEM((LINE, 8, 128), f32),
            dma((2,)),
            dma((2,)),
            dma,
            dma((n,)),
            dma,
            dma,
            dma,
            dma,
            dma,
            dma((n,)),
            dma,
            dma,
            dma,
            dma,
            dma((2, STOPS - 1, 2)),
            dma((2, STOPS - 1, 2)),
            dma,
            dma,
            dma((3,)),
            dma((3,)),
        ],
        compiler_params=pltpu.CompilerParams(
            collective_id=0, has_side_effects=True, vmem_limit_bytes=60 * MIB
        ),
        name="contrastive",
    )(q_hidden, p_hidden, gain.reshape(1, width), idx)


def local(query_hidden, passage_hidden, norm_gain, negatives):
    query_grad, passage_grad, loss, gain_grad = run(query_hidden[0], passage_hidden[0], norm_gain, negatives[0].T)
    return (query_grad[None], passage_grad[None], loss, gain_grad.reshape(norm_gain.shape))


def solution(mesh):
    return jax.shard_map(
        local,
        mesh=mesh,
        in_specs=(P("rep", "batch", None), P("rep", "batch", None), P(), P("rep", "batch", None)),
        out_specs=(P("rep", "batch", None), P("rep", "batch", None), P("rep", "batch"), P()),
        check_vma=False,
    )
```

time: 248 us -> 257 us (1.036)
  Pallas kernels: 238 us -> 250 us
  other arithmetic: 2.94 us -> 0 us
    pallas_call x1, Pallas kernels: 238 us -> 250 us  [run(): pl.pallas_call(functools.partial(kernel, n, reps), in_specs=[hbm, hbm, vm...]
where the time goes in v4:
time: 257 us
  Pallas kernels  250 us (97%)
  local copies, waits for them, and re-layouts  6.97 us (3%)
    pallas_call x1, Pallas kernels, run(): pl.pallas_call(functools.partial(kernel, n, reps), in_specs=[hbm, hbm, vm...  250 us
    unnamed x11, local copies, waits for them, and re-layouts  6.97 us

profile of v4, /device:TPU:1, one launch (start us, length us, event | category | flops | bytes accessed | tf_op | source)
XLA Modules:
  0.0 257.1 jit_solution(15709489694261057019)
XLA Ops:
  0.6 1.3 copy.10
  1.9 249.5 %contrastive.1 = (f32[128,4096]{1,0:T(8,128)}, f32[128,4096]{1,0:T(8,128)}, f32[1,128]{1,0:T(1,128)}, f32[32,128]{1,0:T(8,128)}) custom-call(bf16[128,4096]{1,0:T(8,128)(2,1)} %bitcast.13, bf16[128,4096]{1,0:T(8,128)(2,1)} %bitcast.14, f32[1,4096]{1,0:T(1,128)} %bitcast.15, s32[3,128]{1,0:T(4,128)} %bitcast.17), custom_call_target="tpu_custom_call" | custom-call | tf_op jit(solution)/shard_map/contrastive/pallas_call | solution.py:487
  251.4 0.0 copy-start
  251.4 3.3 %copy.15 = f32[1,128,4096]{2,1,0:T(8,128)} copy(f32[1,128,4096]{2,1,0:T(8,128)} %bitcast.12) | data formatting | bytes 4194304
  254.7 0.0 copy-done
  254.7 0.0 copy-start.2
  254.7 0.0 copy-start.1
  254.7 1.3 copy.16
  256.0 0.0 copy-done.2
  256.0 0.5 copy.17
  256.5 0.0 copy-done.1
  256.5 0.6 copy.18
Async XLA Ops:
  251.4 3.3 %copy-start = (f32[128,4096]{1,0:T(8,128)S(1)}, f32[128,4096]{1,0:T(8,128)}, u32[]{:S(2)}) copy-start(f32[128,4096]{1,0:T(8,128)} %get-tuple-element.9) | copy-start | bytes 6291460
  254.7 1.3 copy-start.2
  254.7 1.8 copy-start.1

commit v5 on v4

--- a/solution.py
+++ b/solution.py
@@ -13,8 +13,8 @@
 SLOTS = 8
 LINE = 8
 STRIDE, UNSTRIDE = 27, 19
-FIRST_HOP = (22, 27)
-SECOND_HOP = (20, 50)
+PARTS = 4
+SECOND_HOP = (6, 20, 34, 48)
 MIB = 1 << 20
 MESH = pl.DeviceIdType.MESH
 NT = (((1,), (1,)), ((), ()))
@@ -27,15 +27,15 @@
 
 def kernel(
     n, reps, q_hbm, p_hbm, gain_ref, idx_ref, q_out, p_out, loss_ref, gain_out,
-    q_ref, p_ref, q_acc, p_acc, p_win, q_win, x_send, w, yq_send, yq_recv, yp_send, yp_recv, table, sums,
+    q_ref, p_ref, q_acc, p_acc, p_win, q_win, x_send, w, y_send, y_recv, table, sums, q_part,
     idx_all, asks, asks_t, t_send, t_recv, shared, side_send, side_recv, q_norm, p_norm, q_weight, p_weight,
     gain_part, gain_near, gain_far, gain_all,
-    in_sems, out_sems, x_sem, x_sems, idx_sem, idx_got, t_sem, t_got, sh_sem, sh_sems, yq_sem, yq_got, yp_sem, yp_got,
+    in_sems, out_sems, x_sem, x_sems, idx_sem, idx_got, t_sem, t_got, sh_sem, sh_sems, y_sem, y_got,
     chain_sem, chain_got, side_sem, side_got, g_sems, g_got,
 ):
     me, rep = lax.axis_index("batch"), lax.axis_index("rep")
     rows, width = q_ref.shape
-    half = rows // 2
+    half, quarter = rows // 2, rows // PARTS
     neg = 3
     places = n * SLOTS
     tiles = width // 128
@@ -74,39 +74,6 @@
 
     lax.fori_loop(1, n, greet, 0)
     lax.fori_loop(0, (reps - 1) * lines, greet_group, 0)
-    for copy in inputs:
-        copy.wait()
-
-    def normalize(chunk, carry):
-        cut = pl.ds(pl.multiple_of(chunk * 16, 16), 16)
-        units = []
-        for src, win, norm in ((q_ref, q_win, q_norm), (p_ref, p_win, p_norm)):
-            scaled = src[cut, :].astype(jnp.float32) * gain_ref[...]
-            length = jnp.sqrt(jnp.sum(scaled * scaled, axis=-1, keepdims=True) + EPS)
-            unit = scaled * (1.0 / length)
-            win[0, cut, :] = unit.astype(jnp.bfloat16)
-            norm[cut, :] = jnp.broadcast_to(1.0 / length, (16, 128))
-            units.append(unit)
-        low = lax.broadcasted_iota(jnp.int32, (16, 128), 1) < 64
-        for tile in range(tiles):
-            q_tile = units[0][:, tile * 128 : (tile + 1) * 128]
-            p_tile = units[1][:, tile * 128 : (tile + 1) * 128]
-            x_send[2 * tile, cut, :] = jnp.where(low, q_tile, pltpu.roll(p_tile, 64, 1)).astype(jnp.bfloat16)
-            x_send[2 * tile + 1, cut, :] = jnp.where(low, pltpu.roll(q_tile, 64, 1), p_tile).astype(jnp.bfloat16)
-        return carry
-
-    lax.fori_loop(0, rows // 16, normalize, 0)
-    w[0] = x_send[me]
-    pl.semaphore_wait(barrier, n - 1 + (reps - 1) * lines)
-
-    def x_copy(i):
-        return remote(x_send.at[ahead(i)], w.at[i], x_sem, x_sems.at[i], ahead(i))
-
-    def start_x(i, carry):
-        x_copy(i).start()
-        return carry
-
-    lax.fori_loop(1, n, start_x, 0)
 
     flat = idx_ref[...]
     flat_f = flat.astype(jnp.float32)
@@ -145,16 +112,50 @@
     idx_all[0] = jnp.concatenate(lines_of, axis=0).astype(jnp.bfloat16)
     own_entry = flat == me * rows + lax.broadcasted_iota(jnp.int32, flat.shape, 1)
 
+    for copy in inputs:
+        copy.wait()
+
+    def normalize(chunk, carry):
+        cut = pl.ds(pl.multiple_of(chunk * 16, 16), 16)
+        units = []
+        for src, win, norm in ((q_ref, q_win, q_norm), (p_ref, p_win, p_norm)):
+            scaled = src[cut, :].astype(jnp.float32) * gain_ref[...]
+            length = jnp.sqrt(jnp.sum(scaled * scaled, axis=-1, keepdims=True) + EPS)
+            unit = scaled * (1.0 / length)
+            win[0, cut, :] = unit.astype(jnp.bfloat16)
+            norm[cut, :] = jnp.broadcast_to(1.0 / length, (16, 128))
+            units.append(unit)
+        low = lax.broadcasted_iota(jnp.int32, (16, 128), 1) < 64
+        for tile in range(tiles):
+            q_tile = units[0][:, tile * 128 : (tile + 1) * 128]
+            p_tile = units[1][:, tile * 128 : (tile + 1) * 128]
+            x_send[2 * tile, cut, :] = jnp.where(low, q_tile, pltpu.roll(p_tile, 64, 1)).astype(jnp.bfloat16)
+            x_send[2 * tile + 1, cut, :] = jnp.where(low, pltpu.roll(q_tile, 64, 1), p_tile).astype(jnp.bfloat16)
+        return carry
+
+    lax.fori_loop(0, rows // 16, normalize, 0)
+    w[0] = x_send[me]
+    pl.semaphore_wait(barrier, n - 1 + (reps - 1) * lines)
+
     def start_idx(i, carry):
         remote(idx_all.at[0], idx_all.at[i], idx_sem, idx_got, ahead(i)).start()
         return carry
 
     lax.fori_loop(1, n, start_idx, 0)
 
+    def x_copy(i):
+        return remote(x_send.at[ahead(i)], w.at[i], x_sem, x_sems.at[i], ahead(i))
+
+    def start_x(i, carry):
+        x_copy(i).start()
+        return carry
+
+    lax.fori_loop(1, n, start_x, 0)
+
     right, left = lax.rem(me + 1, n), lax.rem(me + n - 1, n)
 
     def hop(turn, part):
-        cut = pl.ds(part * half, half)
+        cut = pl.ds(part * quarter, quarter)
         sems = [(chain_sem.at[way, turn - 1, part], chain_got.at[way, turn - 1, part]) for way in range(2)]
         return (
             remote(p_win.at[turn - 1, cut], p_win.at[turn, cut], *sems[0], right),
@@ -171,6 +172,9 @@
         if turn + 1 < STOPS:
             start_hop(turn + 1, part)
 
+    for part in range(PARTS):
+        start_hop(1, part)
+
     others = pl.ds(1, n - 1)
 
     def all_others(buffer, send, recv):
@@ -182,12 +186,6 @@
     asks_t[...] = wide.T
 
     def pick(step, carry):
-        for part in range(2):
-
-            @pl.when(step == FIRST_HOP[part] * n // 64)
-            def _():
-                start_hop(1, part)
-
         picked = []
         for part in range(2):
             pos = 2 * step + part
@@ -229,9 +227,9 @@
         return jnp.concatenate(parts + [jnp.zeros((8 - neg, rows), jnp.float32)], axis=0)
 
     def score_step(pos, carry):
-        for part in range(2):
-
-            @pl.when(pos == SECOND_HOP[part] * n // 64)
+        for part in range(PARTS):
+
+            @pl.when(pos == max(1, SECOND_HOP[part] * n // 64))
             def _():
                 pass_on(1, part)
 
@@ -259,8 +257,10 @@
     positive = jnp.sum(jnp.where(eye, own, 0.0), axis=0, keepdims=True)
     exps = [jnp.exp(own), jnp.exp(window_scores(1, 0))]
     pass_on(2, 0)
+    pass_on(2, 1)
     upper = jnp.exp(window_scores(2, 0, (0, half), 2))
-    pass_on(2, 1)
+    pass_on(2, 2)
+    pass_on(2, 3)
     lower = jnp.exp(window_scores(2, 0, (half, half), 2))
     far = jnp.sum(upper[:, rows:], axis=0, keepdims=True) + jnp.sum(lower[:, rows:], axis=0, keepdims=True)
     side_send[...] = jnp.broadcast_to(far, side_send.shape)
@@ -278,6 +278,11 @@
     v = (exp_t[:neg] * inverse).astype(jnp.bfloat16).astype(jnp.float32)
     own_v = jnp.sum(jnp.where(own_entry, v, 0.0), axis=0, keepdims=True)
     v = jnp.where(own_entry, -v, v)
+    merged = [v[k : k + 1] for k in range(neg)]
+    for k in range(neg):
+        for j in range(k + 1, neg):
+            merged[k] = merged[k] + jnp.where(flat[j : j + 1] == flat[k : k + 1], v[j : j + 1], 0.0)
+    v = jnp.concatenate(merged, axis=0)
     shared[0] = jnp.concatenate([v, jnp.broadcast_to(inverse, (8 - neg, rows))], axis=0)
 
     def sh_copy(i):
@@ -297,16 +302,6 @@
             weight = weight + jnp.where(eye, own_v, 0.0)
         q_weight[stop] = weight.T.astype(jnp.bfloat16)
 
-    def yq_copy(pos):
-        return remote(yq_send.at[pos], yq_recv.at[n - pos], yq_sem, yq_got, behind(pos))
-
-    def fold(block, lanes):
-        first, second = block[:half], block[half:]
-        low = lax.broadcasted_iota(jnp.int32, (half, 128), 1) < 64
-        if lanes == 0:
-            return jnp.where(low, first, pltpu.roll(second, 64, 1)).astype(jnp.bfloat16)
-        return jnp.where(low, pltpu.roll(first, 64, 1), second).astype(jnp.bfloat16)
-
     def spread(step, carry):
         grads = []
         for part in range(2):
@@ -319,43 +314,39 @@
             place = lax.broadcasted_iota(jnp.int32, (places, rows), 0)
             slot = places_of(pos)
             weight = jnp.zeros((places, rows), jnp.float32)
-            for k in range(neg):
-                weight = weight + jnp.where(place == slot[k : k + 1], shared[pos, k : k + 1, :], 0.0)
+            for k in reversed(range(neg)):
+                weight = jnp.where(place == slot[k : k + 1], shared[pos, k : k + 1, :], weight)
             q_side = jnp.maximum(weight, 0.0).astype(jnp.bfloat16)
             p_side = jnp.abs(weight).astype(jnp.bfloat16)
-            yq_send[pos] = fold(dot(q_side, table[pos], TN) / TEMP, 64)
-
-            @pl.when(pos > 0)
-            def _():
-                yq_copy(pos).start()
-
+            q_part[pos] = dot(q_side, table[pos], TN)
             grads.append((dot(p_side, w[pos]) / TEMP).reshape(n, SLOTS, 128))
         both = jnp.concatenate(grads, axis=1).astype(jnp.bfloat16)
         sums[:, pl.ds(pl.multiple_of(step * 16, 16), 16), :] = both
         return carry
 
     lax.fori_loop(0, n // 2, spread, 0)
-    yq_recv[0] = yq_send[0]
-
-    def yp_copy(pos):
-        return remote(yp_send.at[pos], yp_recv.at[n - pos], yp_sem, yp_got, behind(pos))
+
+    def y_copy(pos):
+        return remote(y_send.at[pos], y_recv.at[n - pos], y_sem, y_got, behind(pos))
 
     def gather_tile(pos):
         asked = asks_t[pl.ds(behind(pos), 1), :]
         target = lax.broadcasted_iota(jnp.int32, (rows, places), 0).astype(jnp.float32)
         hot = jnp.where(target == asked, 1.0, 0.0).astype(jnp.bfloat16)
-        return fold(dot(hot, sums[pos]), 0)
+        p_grad = dot(hot, sums[pos])
+        lane = lax.broadcasted_iota(jnp.int32, p_grad.shape, 1)
+        return jnp.where(lane < 64, p_grad, q_part[pos] / TEMP).astype(jnp.bfloat16)
 
     def gather_step(pos, carry):
-        yp_send[pos] = gather_tile(pos)
-        yp_copy(pos).start()
+        y_send[pos] = gather_tile(pos)
+        y_copy(pos).start()
         return carry
 
     lax.fori_loop(1, n, gather_step, 0)
-    yp_recv[0] = gather_tile(0)
-
-    pass_on(3, 0)
-    pass_on(3, 1)
+    y_recv[0] = gather_tile(0)
+
+    for part in range(PARTS):
+        pass_on(3, part)
 
     def inverse_of(stop):
         return shared[position(lax.rem(me + stop, n)), neg : neg + 1, :]
@@ -377,34 +368,31 @@
 
     lax.fori_loop(0, width // 256, products, 0)
 
-    all_others(yq_recv, yq_sem, yq_got).wait_recv()
-    all_others(yp_recv, yp_sem, yp_got).wait_recv()
+    all_others(y_recv, y_sem, y_got).wait_recv()
 
     def finish(chunk, total):
         cut = pl.ds(pl.multiple_of(chunk * 16, 16), 16)
-        upper_cut = pl.ds(pl.multiple_of(half + chunk * 16, 16), 16)
         low = lax.broadcasted_iota(jnp.int32, (16, 128), 1) < 64
-        for src, norm, recv, out in ((q_ref, q_norm, yq_recv, q_acc), (p_ref, p_norm, yp_recv, p_acc)):
-            for tile in range(tiles):
-                lanes = slice(tile * 128, (tile + 1) * 128)
-                even = recv[position(2 * tile), cut, :].astype(jnp.float32)
-                odd = recv[position(2 * tile + 1), cut, :].astype(jnp.float32)
-                out[cut, lanes] += jnp.where(low, even, pltpu.roll(odd, 64, 1))
-                out[upper_cut, lanes] += jnp.where(low, pltpu.roll(even, 64, 1), odd)
-            for here in (cut, upper_cut):
-                hidden = src[here, :].astype(jnp.float32)
-                over = norm[here, :1]
-                gain = gain_ref[...]
-                unit = hidden * gain * over
-                grad = out[here, :]
-                inner = jnp.sum(unit * grad, axis=-1, keepdims=True)
-                scaled = (grad - unit * inner) * over
-                out[here, :] = scaled * gain
-                each = hidden * scaled
-                total = total + each[:8] + each[8:]
+        for tile in range(tiles):
+            lanes = slice(tile * 128, (tile + 1) * 128)
+            even = y_recv[position(2 * tile), cut, :].astype(jnp.float32)
+            odd = y_recv[position(2 * tile + 1), cut, :].astype(jnp.float32)
+            p_acc[cut, lanes] += jnp.where(low, even, pltpu.roll(odd, 64, 1))
+            q_acc[cut, lanes] += jnp.where(low, pltpu.roll(even, 64, 1), odd)
+        for src, norm, out in ((q_ref, q_norm, q_acc), (p_ref, p_norm, p_acc)):
+            hidden = src[cut, :].astype(jnp.float32)
+            over = norm[cut, :1]
+            gain = gain_ref[...]
+            unit = hidden * gain * over
+            grad = out[cut, :]
+            inner = jnp.sum(unit * grad, axis=-1, keepdims=True)
+            scaled = (grad - unit * inner) * over
+            out[cut, :] = scaled * gain
+            each = hidden * scaled
+            total = total + each[:8] + each[8:]
         return total
 
-    total = lax.fori_loop(0, half // 16, finish, jnp.zeros((8, width), jnp.float32))
+    total = lax.fori_loop(0, rows // 16, finish, jnp.zeros((8, width), jnp.float32))
 
     total = jnp.sum(total, axis=0, keepdims=True)
     each = max(1, tiles // LINE)
@@ -463,11 +451,10 @@
     all_others(x_send, x_sem, idx_got).wait_send()
     all_others(t_send, t_sem, t_got).wait_send()
     all_others(shared, sh_sem, idx_got).wait_send()
-    all_others(yq_send, yq_sem, yq_got).wait_send()
-    all_others(yp_send, yp_sem, yp_got).wait_send()
+    all_others(y_send, y_sem, y_got).wait_send()
     side.wait_send()
     for turn in range(1, STOPS):
-        for part in range(2):
+        for part in range(PARTS):
             for copy in hop(turn, part):
                 copy.wait_send()
     for turn, buffer in enumerate((gain_near, gain_far, gain_all)):
@@ -503,12 +490,11 @@
             pltpu.VMEM((STOPS, rows, width), bf16),
             pltpu.VMEM((n, rows, 128), bf16),
             pltpu.VMEM((n, rows, 128), bf16),
-            pltpu.VMEM((n, half, 128), bf16),
-            pltpu.VMEM((n, half, 128), bf16),
-            pltpu.VMEM((n, half, 128), bf16),
-            pltpu.VMEM((n, half, 128), bf16),
+            pltpu.VMEM((n, rows, 128), bf16),
+            pltpu.VMEM((n, rows, 128), bf16),
             pltpu.VMEM((n, places, 128), bf16),
             pltpu.VMEM((n, places, 128), bf16),
+            pltpu.VMEM((n, rows, 128), f32),
             pltpu.VMEM((n, 2 * SLOTS, 128), bf16),
             pltpu.VMEM((places, 128), bf16),
             pltpu.VMEM((128, places), f32),
@@ -537,10 +523,8 @@
             dma((n,)),
             dma,
             dma,
-            dma,
-            dma,
-            dma((2, STOPS - 1, 2)),
-            dma((2, STOPS - 1, 2)),
+            dma((2, STOPS - 1, PARTS)),
+            dma((2, STOPS - 1, PARTS)),
             dma,
             dma,
             dma((3,)),

time: 257 us -> 243 us (0.946)
  Pallas kernels: 250 us -> 235 us
    pallas_call x1, Pallas kernels: 250 us -> 235 us  [run(): pl.pallas_call(functools.partial(kernel, n, reps), in_specs=[hbm, hbm, vm...]
where the time goes in v5:
time: 243 us
  Pallas kernels  235 us (97%)
  local copies, waits for them, and re-layouts  6.97 us (3%)
    pallas_call x1, Pallas kernels, run(): pl.pallas_call(functools.partial(kernel, n, reps), in_specs=[hbm, hbm, vm...  235 us
    unnamed x11, local copies, waits for them, and re-layouts  6.97 us

profile of v5, /device:TPU:1, one launch (start us, length us, event | category | flops | bytes accessed | tf_op | source)
XLA Modules:
  0.0 242.9 jit_solution(14642173659164396693)
XLA Ops:
  0.6 1.3 copy.10
  1.9 235.3 %contrastive.1 = (f32[128,4096]{1,0:T(8,128)}, f32[128,4096]{1,0:T(8,128)}, f32[1,128]{1,0:T(1,128)}, f32[32,128]{1,0:T(8,128)}) custom-call(bf16[128,4096]{1,0:T(8,128)(2,1)} %bitcast.13, bf16[128,4096]{1,0:T(8,128)(2,1)} %bitcast.14, f32[1,4096]{1,0:T(1,128)} %bitcast.15, s32[3,128]{1,0:T(4,128)} %bitcast.17), custom_call_target="tpu_custom_call" | custom-call | tf_op jit(solution)/shard_map/contrastive/pallas_call | solution.py:474
  237.2 0.0 copy-start
  237.2 3.3 %copy.15 = f32[1,128,4096]{2,1,0:T(8,128)} copy(f32[1,128,4096]{2,1,0:T(8,128)} %bitcast.12) | data formatting | bytes 4194304
  240.5 0.0 copy-done
  240.5 0.0 copy-start.2
  240.5 0.0 copy-start.1
  240.5 1.3 copy.16
  241.8 0.0 copy-done.2
  241.8 0.5 copy.17
  242.3 0.0 copy-done.1
  242.3 0.6 copy.18
Async XLA Ops:
  237.2 3.3 %copy-start = (f32[128,4096]{1,0:T(8,128)S(1)}, f32[128,4096]{1,0:T(8,128)}, u32[]{:S(2)}) copy-start(f32[128,4096]{1,0:T(8,128)} %get-tuple-element.9) | copy-start | bytes 6291460
  240.5 1.3 copy-start.2
  240.5 1.8 copy-start.1

commit v6 on v5

--- a/solution.py
+++ b/solution.py
@@ -166,11 +166,9 @@
         for copy in hop(turn, part):
             copy.start()
 
-    def pass_on(turn, part):
+    def end_hop(turn, part):
         for copy in hop(turn, part):
             copy.wait_recv()
-        if turn + 1 < STOPS:
-            start_hop(turn + 1, part)
 
     for part in range(PARTS):
         start_hop(1, part)
@@ -231,7 +229,8 @@
 
             @pl.when(pos == max(1, SECOND_HOP[part] * n // 64))
             def _():
-                pass_on(1, part)
+                end_hop(1, part)
+                start_hop(2, part)
 
         t_send[pos] = partial_scores(pos)
         t_copy(pos).start()
@@ -256,11 +255,11 @@
     eye = down == across
     positive = jnp.sum(jnp.where(eye, own, 0.0), axis=0, keepdims=True)
     exps = [jnp.exp(own), jnp.exp(window_scores(1, 0))]
-    pass_on(2, 0)
-    pass_on(2, 1)
+    end_hop(2, 0)
+    end_hop(2, 1)
     upper = jnp.exp(window_scores(2, 0, (0, half), 2))
-    pass_on(2, 2)
-    pass_on(2, 3)
+    end_hop(2, 2)
+    end_hop(2, 3)
     lower = jnp.exp(window_scores(2, 0, (half, half), 2))
     far = jnp.sum(upper[:, rows:], axis=0, keepdims=True) + jnp.sum(lower[:, rows:], axis=0, keepdims=True)
     side_send[...] = jnp.broadcast_to(far, side_send.shape)
@@ -293,6 +292,8 @@
         return carry
 
     lax.fori_loop(1, n, start_sh, 0)
+    for part in range(PARTS):
+        start_hop(3, part)
     loss_ref[...] = jnp.log(partition) - positive
     for stop in range(STOPS - 1):
         weight = exps[stop] * inverse
@@ -346,7 +347,7 @@
     y_recv[0] = gather_tile(0)
 
     for part in range(PARTS):
-        pass_on(3, part)
+        end_hop(3, part)
 
     def inverse_of(stop):
         return shared[position(lax.rem(me + stop, n)), neg : neg + 1, :]

time: 243 us -> 227 us (0.934)
  Pallas kernels: 235 us -> 219 us
    pallas_call x1, Pallas kernels: 235 us -> 219 us  [run(): pl.pallas_call(functools.partial(kernel, n, reps), in_specs=[hbm, hbm, vm...]
where the time goes in v6:
time: 227 us
  Pallas kernels  219 us (96%)
  local copies, waits for them, and re-layouts  6.97 us (3%)
    pallas_call x1, Pallas kernels, run(): pl.pallas_call(functools.partial(kernel, n, reps), in_specs=[hbm, hbm, vm...  219 us
    unnamed x11, local copies, waits for them, and re-layouts  6.97 us

profile of v6, /device:TPU:1, one launch (start us, length us, event | category | flops | bytes accessed | tf_op | source)
XLA Modules:
  0.0 227.1 jit_solution(17404811893314795072)
XLA Ops:
  0.6 1.3 copy.10
  1.9 219.5 %contrastive.1 = (f32[128,4096]{1,0:T(8,128)}, f32[128,4096]{1,0:T(8,128)}, f32[1,128]{1,0:T(1,128)}, f32[32,128]{1,0:T(8,128)}) custom-call(bf16[128,4096]{1,0:T(8,128)(2,1)} %bitcast.13, bf16[128,4096]{1,0:T(8,128)(2,1)} %bitcast.14, f32[1,4096]{1,0:T(1,128)} %bitcast.15, s32[3,128]{1,0:T(4,128)} %bitcast.17), custom_call_target="tpu_custom_call" | custom-call | tf_op jit(solution)/shard_map/contrastive/pallas_call | solution.py:475
  221.4 0.0 copy-start
  221.4 3.3 %copy.15 = f32[1,128,4096]{2,1,0:T(8,128)} copy(f32[1,128,4096]{2,1,0:T(8,128)} %bitcast.12) | data formatting | bytes 4194304
  224.7 0.0 copy-done
  224.7 0.0 copy-start.2
  224.7 0.0 copy-start.1
  224.7 1.3 copy.16
  226.0 0.0 copy-done.2
  226.0 0.5 copy.17
  226.5 0.0 copy-done.1
  226.5 0.6 copy.18
Async XLA Ops:
  221.4 3.3 %copy-start = (f32[128,4096]{1,0:T(8,128)S(1)}, f32[128,4096]{1,0:T(8,128)}, u32[]{:S(2)}) copy-start(f32[128,4096]{1,0:T(8,128)} %get-tuple-element.9) | copy-start | bytes 6291460
  224.7 1.3 copy-start.2
  224.7 1.8 copy-start.1

commit v7 on v6

--- a/solution.py
+++ b/solution.py
@@ -14,7 +14,7 @@
 LINE = 8
 STRIDE, UNSTRIDE = 27, 19
 PARTS = 4
-SECOND_HOP = (6, 20, 34, 48)
+SECOND_HOP = (1, 2, 3, 4)
 MIB = 1 << 20
 MESH = pl.DeviceIdType.MESH
 NT = (((1,), (1,)), ((), ()))

time: 227 us -> 229 us (level)
  Pallas kernels: 219 us -> 222 us
where the time goes in v7:
time: 229 us
  Pallas kernels  222 us (97%)
  local copies, waits for them, and re-layouts  6.97 us (3%)
    pallas_call x1, Pallas kernels, run(): pl.pallas_call(functools.partial(kernel, n, reps), in_specs=[hbm, hbm, vm...  222 us
    unnamed x11, local copies, waits for them, and re-layouts  6.97 us

profile of v7, /device:TPU:1, one launch (start us, length us, event | category | flops | bytes accessed | tf_op | source)
XLA Modules:
  0.0 229.3 jit_solution(8712806633131459297)
XLA Ops:
  0.6 1.3 copy.10
  1.9 221.6 %contrastive.1 = (f32[128,4096]{1,0:T(8,128)}, f32[128,4096]{1,0:T(8,128)}, f32[1,128]{1,0:T(1,128)}, f32[32,128]{1,0:T(8,128)}) custom-call(bf16[128,4096]{1,0:T(8,128)(2,1)} %bitcast.13, bf16[128,4096]{1,0:T(8,128)(2,1)} %bitcast.14, f32[1,4096]{1,0:T(1,128)} %bitcast.15, s32[3,128]{1,0:T(4,128)} %bitcast.17), custom_call_target="tpu_custom_call" | custom-call | tf_op jit(solution)/shard_map/contrastive/pallas_call | solution.py:475
  223.5 0.0 copy-start
  223.5 3.3 %copy.15 = f32[1,128,4096]{2,1,0:T(8,128)} copy(f32[1,128,4096]{2,1,0:T(8,128)} %bitcast.12) | data formatting | bytes 4194304
  226.8 0.0 copy-done
  226.8 0.0 copy-start.2
  226.8 0.0 copy-start.1
  226.8 1.3 copy.16
  228.1 0.0 copy-done.2
  228.1 0.5 copy.17
  228.6 0.0 copy-done.1
  228.6 0.6 copy.18
Async XLA Ops:
  223.5 3.3 %copy-start = (f32[128,4096]{1,0:T(8,128)S(1)}, f32[128,4096]{1,0:T(8,128)}, u32[]{:S(2)}) copy-start(f32[128,4096]{1,0:T(8,128)} %get-tuple-element.9) | copy-start | bytes 6291460
  226.8 1.3 copy-start.2
  226.8 1.8 copy-start.1
